TPU v7x, 32 devices: a whole 2x2x4 slice. The times are simulated.
32 devices in a mesh: gx: 4 (over y, core), gy: 8 (over z, x).
Axes of the slice: x: 2, y: 2, z: 4, core: 2. Of those that a mesh axis runs over, the one named last changes fastest.
Arguments:
- start_vector: float32 [2, 16, 64, 1024], P(None, None, 'gx', 'gy'), may hold values from -6 to 6
- viscosity: float32 [16, 64, 1024], P(None, 'gx', 'gy'), may hold values from 0.1 to 10
- friction: float32 [16, 64, 1024], P(None, 'gx', 'gy'), may hold values from 0.5 to 5
- shifts: float32 [8], replicated, may hold values from 0.2 to 1.6, as said below
Outputs:
- orthonormal: float32 [9, 2, 16, 64, 1024], P(None, None, None, 'gx', 'gy')
- factor: float32 [9, 9], replicated
Inputs may be any that keep to these rules, and one draw needn't show every extreme that they name: The 8 shifts are distinct, one in each of 8 equal parts of the range.
All inputs are finite; a program needn't handle non-finite values.
Results may differ from a plain program's by a relative error of at most 0.00035.
Values sent between devices are 32-bit elements; how exact they have to be, the bound alone decides.
A program may use at most 128 MiB of HBM per device.

v0:
```python
import functools

import jax
import jax.numpy as jnp
from jax import lax
from jax.experimental import pallas as pl
from jax.experimental.pallas import tpu as pltpu
from jax.sharding import PartitionSpec as P

MESH = pl.DeviceIdType.MESH
HALO = 8
GROUP = 2 * HALO
DIRECTIONS = ((1, 0), (-1, 0), (0, 1), (0, -1), (1, 1), (1, -1), (-1, 1), (-1, -1))


def both(lower_ok, upper_ok):
    if lower_ok is None:
        return upper_ok
    if upper_ok is None:
        return lower_ok
    return jnp.logical_and(lower_ok, upper_ok)


def kernel(
    gx_count,
    gy_count,
    start_ref,
    eta_in_ref,
    fric_in_ref,
    shift_ref,
    out_ref,
    factor_ref,
    lower_inv,
    cur,
    eta,
    fric,
    centre_coef,
    a_mid,
    g_mid,
    a_up,
    g_up,
    a_down,
    g_down,
    packed,
    edge,
    red,
    mine_x,
    mine_y,
    slots_x,
    slots_y,
    splat,
    row_send,
    row_recv,
    pack_send,
    pack_recv,
    gx_send,
    gx_recv,
    gy_send,
    gy_recv,
):
    powers = shift_ref.shape[0]
    count = powers + 1
    levels, rows, lanes = eta_in_ref.shape
    wide = rows + 2 * HALO
    me_x, me_y = lax.axis_index("gx"), lax.axis_index("gy")
    total_count = 2.0 * levels * rows * lanes * gx_count * gy_count

    def exists(dx, dy):
        x_ok = {1: me_x < gx_count - 1, -1: me_x > 0, 0: None}[dx]
        y_ok = {1: me_y < gy_count - 1, -1: me_y > 0, 0: None}[dy]
        return both(x_ok, y_ok)

    def device(dx, dy):
        return (jnp.clip(me_x + dx, 0, gx_count - 1), jnp.clip(me_y + dy, 0, gy_count - 1))

    def ring_x(step):
        return (lax.rem(me_x + step, gx_count), me_y)

    def ring_y(step):
        return (me_x, lax.rem(me_y + step, gy_count))

    barrier = pltpu.get_barrier_semaphore()
    for step in range(1, gx_count):
        pl.semaphore_signal(barrier, inc=1, device_id=ring_x(step), device_id_type=MESH)
    for step in range(1, gy_count):
        pl.semaphore_signal(barrier, inc=1, device_id=ring_y(step), device_id_type=MESH)
    for dx, dy in DIRECTIONS[4:]:

        @pl.when(exists(dx, dy))
        def _():
            pl.semaphore_signal(barrier, inc=1, device_id=device(dx, dy), device_id_type=MESH)

    lane = lax.broadcasted_iota(jnp.int32, (wide, lanes), 1)
    row = lax.broadcasted_iota(jnp.int32, (wide, lanes), 0)
    lane_in = lane[:rows]

    def source(field, level):
        if field < 2:
            return start_ref[field, level]
        return (eta_in_ref, fric_in_ref)[field - 2][level]

    for field in range(4):
        for group in range(levels // 8):
            tile = jnp.zeros((rows, lanes), jnp.float32)
            for inner in range(8):
                turned = pltpu.roll(
                    source(field, group * 8 + inner), (GROUP * inner + HALO) % lanes, 1
                )
                tile = jnp.where(lane_in // GROUP == inner, turned, tile)
            packed[field * (levels // 8) + group] = tile

    barrier_x = jnp.where(me_x > 0, 1, 0) + jnp.where(me_x < gx_count - 1, 1, 0)
    barrier_y = jnp.where(me_y > 0, 1, 0) + jnp.where(me_y < gy_count - 1, 1, 0)
    pl.semaphore_wait(barrier, gx_count + gy_count - 2 + barrier_x * barrier_y)

    def row_copies(index):
        dx, dy = DIRECTIONS[index]
        src = pl.ds(rows - HALO, HALO) if dx > 0 else pl.ds(0, HALO)
        dst = pl.ds(0, HALO) if dx > 0 else pl.ds(rows + HALO, HALO)
        inner = pl.ds(1, levels)
        pairs = (
            (start_ref.at[:, :, src], cur.at[0, 0, :, inner, dst]),
            (eta_in_ref.at[:, src], eta.at[0, inner, dst]),
            (fric_in_ref.at[:, src], fric.at[0, :, dst]),
        )
        return [
            pltpu.make_async_remote_copy(
                src_ref=a,
                dst_ref=b,
                send_sem=row_send.at[index, n],
                recv_sem=row_recv.at[index, n],
                device_id=device(dx, dy),
                device_id_type=MESH,
            )
            for n, (a, b) in enumerate(pairs)
        ]

    def pack_copies(index):
        dx, dy = DIRECTIONS[index]
        side = 0 if dy > 0 else 1
        if dx == 0:
            src, dst = pl.ds(0, rows), pl.ds(HALO, rows)
        elif dx > 0:
            src, dst = pl.ds(rows - HALO, HALO), pl.ds(0, HALO)
        else:
            src, dst = pl.ds(0, HALO), pl.ds(rows + HALO, HALO)
        return [
            pltpu.make_async_remote_copy(
                src_ref=packed.at[:, src],
                dst_ref=edge.at[side, :, dst],
                send_sem=pack_send.at[index - 2],
                recv_sem=pack_recv.at[index - 2],
                device_id=device(dx, dy),
                device_id_type=MESH,
            )
        ]

    def copies(index):
        return row_copies(index) if index < 2 else pack_copies(index)

    for index, (dx, dy) in enumerate(DIRECTIONS):

        @pl.when(exists(dx, dy))
        def _():
            for copy in copies(index):
                copy.start()

    zero_tile = jnp.zeros((wide, lanes), jnp.float32)
    for comp in range(2):
        for tile in range(2):
            for slot in range(2):
                cur[slot, tile, comp, 0] = zero_tile
                cur[slot, tile, comp, levels + 1] = zero_tile
        cur[0, 0, comp, 1 : levels + 1, HALO : HALO + rows] = start_ref[comp]
        out_ref[0, comp] = start_ref[comp]
    for tile in range(2):
        eta[tile, 0] = zero_tile
        eta[tile, levels + 1] = zero_tile
    eta[0, 1 : levels + 1, HALO : HALO + rows] = eta_in_ref[...]
    fric[0, :, HALO : HALO + rows] = fric_in_ref[...]
    for index, (dx, dy) in enumerate(DIRECTIONS):
        here = exists(-dx, -dy)

        @pl.when(jnp.logical_not(here))
        def _():
            start = 0 if dx > 0 else (HALO if dx == 0 else rows + HALO)
            size = rows if dx == 0 else HALO
            if dy == 0:
                blank = jnp.zeros((levels, HALO, lanes), jnp.float32)
                for comp in range(2):
                    cur[0, 0, comp, 1 : levels + 1, start : start + size] = blank
                eta[0, 1 : levels + 1, start : start + size] = blank
                fric[0, :, start : start + size] = blank
            else:
                side = 0 if dy > 0 else 1
                edge[side, :, start : start + size] = jnp.zeros(
                    (edge.shape[1], size, lanes), jnp.float32
                )

        @pl.when(here)
        def _():
            for copy in copies(index):
                copy.wait_recv()

    is_edge = (lane < HALO) | (lane >= lanes - HALO)
    for field in range(4):
        for group in range(levels // 8):
            spot = field * (levels // 8) + group
            merged = jnp.where(lane % GROUP >= HALO, edge[1, spot], edge[0, spot])
            for inner in range(8):
                level = group * 8 + inner
                turned = pltpu.roll(merged, (2 * lanes - GROUP * inner - HALO) % lanes, 1)
                turned = jnp.where(is_edge, turned, 0.0)
                if field < 2:
                    cur[0, 1, field, level + 1] = turned
                elif field == 2:
                    eta[1, level + 1] = turned
                else:
                    fric[1, level] = turned

    def from_next(first, second):
        a, b = pltpu.roll(first, lanes - 1, 1), pltpu.roll(second, lanes - 1, 1)
        at_end = lane[: first.shape[0]] == lanes - 1
        return jnp.where(at_end, b, a), jnp.where(at_end, a, b)

    def from_last(first, second):
        a, b = pltpu.roll(first, 1, 1), pltpu.roll(second, 1, 1)
        at_start = lane[: first.shape[0]] == 0
        return jnp.where(at_start, b, a), jnp.where(at_start, a, b)

    def smooth_rows(value):
        pair = value + pltpu.roll(value, wide - 1, 0)
        return pair + pltpu.roll(pair, 1, 0)

    row_ok = ((row >= HALO) | (me_x > 0)) & ((row < HALO + rows) | (me_x < gx_count - 1))
    side_ok = ((lane < HALO) & (me_y < gy_count - 1)) | ((lane >= lanes - HALO) & (me_y > 0))
    inside = (row_ok, row_ok & side_ok)

    def coefficients(level, carry):
        sums = [
            smooth_rows(eta[t, level] + 2.0 * eta[t, level + 1] + eta[t, level + 2])
            for t in range(2)
        ]
        after, before = from_next(*sums), from_last(*sums)
        a_pair, g_pair = [], []
        for t in range(2):
            here = eta[t, level + 1]
            diagonal = (
                fric[t, level] + 6.0 * here + 0.125 * (2.0 * sums[t] + after[t] + before[t])
            )
            inverse = jnp.where(inside[t], 0.125 / jnp.where(inside[t], diagonal, 1.0), 0.0)
            a_pair.append(here * inverse)
            g_pair.append(inverse)
            centre_coef[t, level] = 1.0 + 16.0 * a_pair[t]
            a_mid[t, level] = 2.0 * a_pair[t]
            g_mid[t, level] = 2.0 * g_pair[t]
        for values, up, down in ((a_pair, a_up, a_down), (g_pair, g_up, g_down)):
            ahead, behind = from_last(*values), from_next(*values)
            for t in range(2):
                up[t, level] = ahead[t]
                down[t, level] = behind[t]
        return carry

    lax.fori_loop(0, levels, coefficients, 0)

    def power_step(power, carry, final=False):
        kept = slice(HALO, HALO + rows) if final else slice(0, wide)

        slot = power % 2
        newton = shift_ref[power]

        def level_step(level, inner_carry):
            crossed = [[None, None], [None, None]]
            for t in range(2):
                for comp in range(2):
                    value = cur[slot, t, comp, level + 1]
                    slope = pltpu.roll(value, wide - 1, 0) - pltpu.roll(value, 1, 0)
                    crossed[comp][t] = (slope + slope)[kept]
            for comp in range(2):
                centre, ups, downs = [], [], []
                for t in range(2):
                    below = cur[slot, t, comp, level]
                    value = cur[slot, t, comp, level + 1]
                    above = cur[slot, t, comp, level + 2]
                    plain = smooth_rows(below + 2.0 * value + above)[kept]
                    scaled = smooth_rows(
                        eta[t, level] * below
                        + 2.0 * (eta[t, level + 1] * value)
                        + eta[t, level + 2] * above
                    )[kept]
                    cross = crossed[1 - comp][t]
                    centre.append(
                        (centre_coef[t, level, kept] - newton) * value[kept]
                        - (a_mid[t, level, kept] * plain + g_mid[t, level, kept] * scaled)
                    )
                    ups.append(a_up[t, level, kept] * (plain - cross) + g_up[t, level, kept] * scaled)
                    downs.append(a_down[t, level, kept] * (plain + cross) + g_down[t, level, kept] * scaled)
                after, before = from_next(*ups), from_last(*downs)
                for t in range(2):
                    result = centre[t] - (after[t] + before[t])
                    if not final:
                        cur[1 - slot, t, comp, level + 1] = result
                    if final and t == 0:
                        out_ref[power + 1, comp, level] = result
                    elif t == 0:
                        out_ref[power + 1, comp, level] = result[HALO : HALO + rows]
            return inner_carry

        return lax.fori_loop(0, levels, level_step, carry)

    lax.fori_loop(0, powers - 1, power_step, 0)
    power_step(powers - 1, 0, final=True)

    pairs = [(i, j) for i in range(count) for j in range(i + 1)]
    place = {pair: n for n, pair in enumerate(pairs)}
    tiles = (len(pairs) + 7) // 8
    lane_8 = lax.broadcasted_iota(jnp.int32, (8, lanes), 1)

    def add_products(sums, vectors):
        return tuple(total + vectors[i] * vectors[j] for total, (i, j) in zip(sums, pairs))

    zeros = tuple(jnp.zeros((8, lanes), jnp.float32) for _ in pairs)

    def exchange(phase, mine, slots, sends, recvs, me, peers, target):
        copies_out = []
        for step in range(1, peers):
            copy = pltpu.make_async_remote_copy(
                src_ref=mine.at[phase],
                dst_ref=slots.at[phase, me],
                send_sem=sends.at[phase, step],
                recv_sem=recvs.at[phase, step],
                device_id=target(step),
                device_id_type=MESH,
            )
            copy.start()
            copies_out.append(copy)
        slots[phase, me] = mine[phase]
        for copy in copies_out:
            copy.wait()
        total = slots[phase, 0]
        for peer in range(1, peers):
            total = total + slots[phase, peer]
        return total

    def gram_of(sums, phase):
        red[8 * tiles - 8 : 8 * tiles] = jnp.zeros((8, lanes), jnp.float32)
        for n, total in enumerate(sums):
            red[n : n + 1] = jnp.sum(total, axis=0, keepdims=True)
        summed = jnp.sum(red[...], axis=1, keepdims=True)
        tile = jnp.zeros((8, lanes), jnp.float32)
        for t in range(tiles):
            tile = jnp.where(lane_8 == t, summed[8 * t : 8 * t + 8], tile)
        mine_x[phase] = tile
        mine_y[phase] = exchange(
            phase, mine_x, slots_x, gx_send, gx_recv, me_x, gx_count, ring_x
        )
        whole = exchange(phase, mine_y, slots_y, gy_send, gy_recv, me_y, gy_count, ring_y)
        whole = whole / total_count
        for t in range(tiles):
            splat[8 * t : 8 * t + 8] = jnp.broadcast_to(whole[:, t : t + 1], (8, lanes))
        return {pair: splat[n : n + 1] for n, pair in enumerate(pairs)}

    def factorise(gram):
        left = dict(gram)
        low, inv = {}, {}
        for j in range(count):
            root = jnp.sqrt(left[j, j])
            scale = 1.0 / root
            low[j, j], inv[j, j] = root, scale
            for i in range(j + 1, count):
                low[i, j] = left[i, j] * scale
            for i in range(j + 1, count):
                for k in range(j + 1, i + 1):
                    left[i, k] = left[i, k] - low[i, j] * low[k, j]
        for i in range(count):
            for j in range(i):
                total = low[i, j] * inv[j, j]
                for k in range(j + 1, i):
                    total = total + low[i, k] * inv[k, j]
                inv[i, j] = -(total * inv[i, i])
        for pair, n in place.items():
            lower_inv[n : n + 1] = inv[pair]
        return low

    def combine(vectors):
        results = []
        for i in range(count):
            total = lower_inv[place[i, 0] : place[i, 0] + 1] * vectors[0]
            for j in range(1, i + 1):
                total = total + lower_inv[place[i, j] : place[i, j] + 1] * vectors[j]
            results.append(total)
        return results

    def basis_at(spot, half):
        comp, level = spot // levels, lax.rem(spot, levels)
        return [out_ref[n, comp, level, 8 * half : 8 * half + 8] for n in range(count)]

    def gram_step(spot, sums):
        for half in range(rows // 8):
            sums = add_products(sums, basis_at(spot, half))
        return sums

    low_one = factorise(gram_of(lax.fori_loop(0, 2 * levels, gram_step, zeros), 0))

    def ortho_step(spot, sums):
        comp, level = spot // levels, lax.rem(spot, levels)
        for half in range(rows // 8):
            vectors = combine(basis_at(spot, half))
            for n in range(count):
                out_ref[n, comp, level, 8 * half : 8 * half + 8] = vectors[n]
            sums = add_products(sums, vectors)
        return sums

    low_two = factorise(gram_of(lax.fori_loop(0, 2 * levels, ortho_step, zeros), 1))

    fac_row = lax.broadcasted_iota(jnp.int32, (count, count), 0)
    fac_col = lax.broadcasted_iota(jnp.int32, (count, count), 1)
    factor = jnp.zeros((count, count), jnp.float32)
    for i in range(count):
        for j in range(i, count):
            total = low_two[i, i] * low_one[j, i]
            for k in range(i + 1, j + 1):
                total = total + low_two[k, i] * low_one[j, k]
            factor = jnp.where((fac_row == i) & (fac_col == j), total[:, :count], factor)
    factor_ref[...] = factor

    for index, (dx, dy) in enumerate(DIRECTIONS):

        @pl.when(exists(dx, dy))
        def _():
            for copy in copies(index):
                copy.wait_send()


def finish(inverse_ref, basis_ref, out_ref):
    count, _, depth, rows, _ = out_ref.shape
    comp, first = pl.program_id(0), pl.program_id(1) * depth

    def one_level(level, carry):
        for half in range(rows // 8):
            part = slice(8 * half, 8 * half + 8)
            vectors = [basis_ref[n, comp, first + level, part] for n in range(count)]
            spot = 0
            for i in range(count):
                total = inverse_ref[spot : spot + 1] * vectors[0]
                for j in range(1, i + 1):
                    total = total + inverse_ref[spot + j : spot + j + 1] * vectors[j]
                out_ref[i, 0, level, part] = total
                spot += i + 1
        return carry

    lax.fori_loop(0, depth, one_level, 0)


def on_device(gx_count, gy_count, start_vector, viscosity, friction, shifts):
    levels, rows, lanes = viscosity.shape
    count = shifts.shape[0] + 1
    wide = rows + 2 * HALO
    tiles = (count * (count + 1) // 2 + 7) // 8
    f32 = jnp.float32
    coef = pltpu.VMEM((2, levels, wide, lanes), f32)
    dma = pltpu.SemaphoreType.DMA
    vmem = pl.BlockSpec(memory_space=pltpu.VMEM)
    ortho_one, factor, inverse = pl.pallas_call(
        functools.partial(kernel, gx_count, gy_count),
        out_shape=(
            jax.ShapeDtypeStruct((count,) + start_vector.shape, f32),
            jax.ShapeDtypeStruct((count, count), f32),
            jax.ShapeDtypeStruct((8 * tiles, lanes), f32),
        ),
        in_specs=[vmem, vmem, vmem, pl.BlockSpec(memory_space=pltpu.SMEM)],
        out_specs=(vmem, vmem, vmem),
        scratch_shapes=[
            pltpu.VMEM((2, 2, 2, levels + 2, wide, lanes), f32),
            pltpu.VMEM((2, levels + 2, wide, lanes), f32),
            coef,
            coef,
            coef,
            coef,
            coef,
            coef,
            coef,
            coef,
            pltpu.VMEM((levels // 2, rows, lanes), f32),
            pltpu.VMEM((2, levels // 2, wide, lanes), f32),
            pltpu.VMEM((8 * tiles, lanes), f32),
            pltpu.VMEM((2, 8, lanes), f32),
            pltpu.VMEM((2, 8, lanes), f32),
            pltpu.VMEM((2, gx_count, 8, lanes), f32),
            pltpu.VMEM((2, gy_count, 8, lanes), f32),
            pltpu.VMEM((8 * tiles, lanes), f32),
            dma((2, 3)),
            dma((2, 3)),
            dma((6,)),
            dma((6,)),
            dma((2, gx_count)),
            dma((2, gx_count)),
            dma((2, gy_count)),
            dma((2, gy_count)),
        ],
        compiler_params=pltpu.CompilerParams(
            collective_id=0, has_side_effects=True, vmem_limit_bytes=40 * 2**20
        ),
    )(start_vector, viscosity, friction, shifts)
    depth = 8 if levels % 8 == 0 else 1
    block = pl.BlockSpec((count, 1, depth, rows, lanes), lambda c, z: (0, c, z, 0, 0))
    orthonormal = pl.pallas_call(
        finish,
        grid=(2, levels // depth),
        out_shape=jax.ShapeDtypeStruct(ortho_one.shape, f32),
        in_specs=[vmem, vmem],
        compiler_params=pltpu.CompilerParams(vmem_limit_bytes=12 * 2**20),
        out_specs=block,
    )(inverse, ortho_one)
    return orthonormal, factor


def solution(mesh):
    return jax.shard_map(
        functools.partial(on_device, mesh.shape["gx"], mesh.shape["gy"]),
        mesh=mesh,
        in_specs=(P(None, None, "gx", "gy"), P(None, "gx", "gy"), P(None, "gx", "gy"), P()),
        out_specs=(P(None, None, None, "gx", "gy"), P()),
        check_vma=False,
    )
```

profile of v0, /device:TPU:0, one launch (start us, length us, event | category | flops | bytes accessed | tf_op | source)
XLA Modules:
  0.0 69.6 jit_solution(7102850413619591499)
XLA Ops:
  0.6 0.0 copy-start
  0.6 0.9 %copy-done = f32[2,16,16,128]{3,2,1,0:T(8,128)S(1)} copy-done((f32[2,16,16,128]{3,2,1,0:T(8,128)S(1)}, f32[2,16,16,128]{3,2,1,0:T(8,128)}, u32[]{:S(2)}) %copy-start) | copy-done | bytes 262168
  1.6 0.0 copy-start.1
  1.6 0.9 %copy-done.1 = f32[16,16,128]{2,1,0:T(8,128)S(1)} copy-done((f32[16,16,128]{2,1,0:T(8,128)S(1)}, f32[16,16,128]{2,1,0:T(8,128)}, u32[]{:S(2)}) %copy-start.1) | copy-done | bytes 131096
  2.5 0.0 copy-start.2
  2.5 0.9 %copy-done.2 = f32[16,16,128]{2,1,0:T(8,128)S(1)} copy-done((f32[16,16,128]{2,1,0:T(8,128)S(1)}, f32[16,16,128]{2,1,0:T(8,128)}, u32[]{:S(2)}) %copy-start.2) | copy-done | bytes 131096
  3.4 0.0 copy-start.3
  3.4 0.7 copy-done.3
  4.0 62.5 %shard_map.59 = (f32[9,2,16,16,128]{4,3,2,1,0:T(8,128)S(1)}, f32[9,9]{1,0:T(8,128)S(1)}, f32[48,128]{1,0:T(8,128)S(1)}) custom-call(f32[2,16,16,128]{3,2,1,0:T(8,128)S(1)} %copy-done, f32[16,16,128]{2,1,0:T(8,128)S(1)} %copy-done.1, f32[16,16,128]{2,1,0:T(8,128)S(1)} %copy-done.2, f32[8]{0:T(128)S(1)} %copy-done.3), custom_call_target="tpu_custom_call" | custom-call | tf_op jit(solution)/shard_map/pallas_call | solution.py:464
  66.5 2.5 %shard_map.60 = f32[9,2,16,16,128]{4,3,2,1,0:T(8,128)} custom-call(f32[48,128]{1,0:T(8,128)S(1)} %get-tuple-element.5.inverse_ref, f32[9,2,16,16,128]{4,3,2,1,0:T(8,128)S(1)} %get-tuple-element.6.basis_ref), custom_call_target="tpu_custom_call" | custom-call | tf_op jit(solution)/shard_map/pallas_call | solution.py:507
  69.0 0.6 copy.7
Async XLA Ops:
  0.6 1.0 %copy-start = (f32[2,16,16,128]{3,2,1,0:T(8,128)S(1)}, f32[2,16,16,128]{3,2,1,0:T(8,128)}, u32[]{:S(2)}) copy-start(f32[2,16,16,128]{3,2,1,0:T(8,128)} %start_ref.1) | copy-start | bytes 786436
  1.6 0.9 %copy-start.1 = (f32[16,16,128]{2,1,0:T(8,128)S(1)}, f32[16,16,128]{2,1,0:T(8,128)}, u32[]{:S(2)}) copy-start(f32[16,16,128]{2,1,0:T(8,128)} %eta_in_ref.1) | copy-start | bytes 393220
  2.5 0.9 %copy-start.2 = (f32[16,16,128]{2,1,0:T(8,128)S(1)}, f32[16,16,128]{2,1,0:T(8,128)}, u32[]{:S(2)}) copy-start(f32[16,16,128]{2,1,0:T(8,128)} %fric_in_ref.1) | copy-start | bytes 393220
  3.4 0.7 copy-start.3
where the time goes:
time: 69.8 us; the launch traced here: 69.6 us
  Pallas kernels  64.9 us (93%)
  local copies, waits for them, and re-layouts  4 us (6%)
    pallas_call x1, Pallas kernels, on_device(): pl.pallas_call(functools.partial(kernel, gx_count, gy_count), out_shape=(...  62.5 us
    unnamed x9, local copies, waits for them, and re-layouts  4 us
    pallas_call x1, Pallas kernels, on_device(): pl.pallas_call(finish, grid=(2, levels // depth), out_shape=jax.ShapeDtyp...  2.46 us

commit v1 on v0

--- a/solution.py
+++ b/solution.py
@@ -24,13 +24,18 @@
 def kernel(
     gx_count,
     gy_count,
+    start_hbm,
+    eta_hbm,
+    fric_hbm,
+    shift_hbm,
+    out_ref,
+    factor_ref,
+    lower_inv,
     start_ref,
     eta_in_ref,
     fric_in_ref,
     shift_ref,
-    out_ref,
-    factor_ref,
-    lower_inv,
+    load_sem,
     cur,
     eta,
     fric,
@@ -44,21 +49,17 @@
     packed,
     edge,
     red,
-    mine_x,
-    mine_y,
-    slots_x,
-    slots_y,
+    mine,
+    slots,
     splat,
     row_send,
     row_recv,
     pack_send,
     pack_recv,
-    gx_send,
-    gx_recv,
-    gy_send,
-    gy_recv,
+    gram_send,
+    gram_recv,
 ):
-    powers = shift_ref.shape[0]
+    powers = shift_hbm.shape[0]
     count = powers + 1
     levels, rows, lanes = eta_in_ref.shape
     wide = rows + 2 * HALO
@@ -73,22 +74,31 @@
     def device(dx, dy):
         return (jnp.clip(me_x + dx, 0, gx_count - 1), jnp.clip(me_y + dy, 0, gy_count - 1))
 
-    def ring_x(step):
-        return (lax.rem(me_x + step, gx_count), me_y)
-
-    def ring_y(step):
-        return (me_x, lax.rem(me_y + step, gy_count))
+    devices = gx_count * gy_count
+    me = me_x * gy_count + me_y
+
+    def peer(step):
+        other = lax.rem(me + step, devices)
+        return (lax.div(other, gy_count), lax.rem(other, gy_count))
 
     barrier = pltpu.get_barrier_semaphore()
-    for step in range(1, gx_count):
-        pl.semaphore_signal(barrier, inc=1, device_id=ring_x(step), device_id_type=MESH)
-    for step in range(1, gy_count):
-        pl.semaphore_signal(barrier, inc=1, device_id=ring_y(step), device_id_type=MESH)
-    for dx, dy in DIRECTIONS[4:]:
-
-        @pl.when(exists(dx, dy))
-        def _():
-            pl.semaphore_signal(barrier, inc=1, device_id=device(dx, dy), device_id_type=MESH)
+    for step in range(1, devices):
+        pl.semaphore_signal(barrier, inc=1, device_id=peer(step), device_id_type=MESH)
+    loads = [
+        pltpu.make_async_copy(src, dst, load_sem.at[n])
+        for n, (src, dst) in enumerate(
+            (
+                (start_hbm, start_ref),
+                (eta_hbm, eta_in_ref),
+                (fric_hbm, fric_in_ref),
+                (shift_hbm, shift_ref),
+            )
+        )
+    ]
+    for load in loads:
+        load.start()
+    for load in loads:
+        load.wait()
 
     lane = lax.broadcasted_iota(jnp.int32, (wide, lanes), 1)
     row = lax.broadcasted_iota(jnp.int32, (wide, lanes), 0)
@@ -109,9 +119,7 @@
                 tile = jnp.where(lane_in // GROUP == inner, turned, tile)
             packed[field * (levels // 8) + group] = tile
 
-    barrier_x = jnp.where(me_x > 0, 1, 0) + jnp.where(me_x < gx_count - 1, 1, 0)
-    barrier_y = jnp.where(me_y > 0, 1, 0) + jnp.where(me_y < gy_count - 1, 1, 0)
-    pl.semaphore_wait(barrier, gx_count + gy_count - 2 + barrier_x * barrier_y)
+    pl.semaphore_wait(barrier, devices - 1)
 
     def row_copies(index):
         dx, dy = DIRECTIONS[index]
@@ -313,51 +321,52 @@
 
     pairs = [(i, j) for i in range(count) for j in range(i + 1)]
     place = {pair: n for n, pair in enumerate(pairs)}
-    tiles = (len(pairs) + 7) // 8
-    lane_8 = lax.broadcasted_iota(jnp.int32, (8, lanes), 1)
+    padded = red.shape[0]
+    red[...] = jnp.zeros((padded, lanes), jnp.float32)
+    ones = jnp.ones((8, lanes), jnp.float32)
+    splat_rows = splat.shape[0]
+    diagonal = lax.broadcasted_iota(jnp.int32, (splat_rows, lanes), 1) == lax.broadcasted_iota(
+        jnp.int32, (splat_rows, lanes), 0
+    )
 
     def add_products(sums, vectors):
         return tuple(total + vectors[i] * vectors[j] for total, (i, j) in zip(sums, pairs))
 
     zeros = tuple(jnp.zeros((8, lanes), jnp.float32) for _ in pairs)
 
-    def exchange(phase, mine, slots, sends, recvs, me, peers, target):
-        copies_out = []
-        for step in range(1, peers):
-            copy = pltpu.make_async_remote_copy(
-                src_ref=mine.at[phase],
-                dst_ref=slots.at[phase, me],
-                send_sem=sends.at[phase, step],
-                recv_sem=recvs.at[phase, step],
-                device_id=target(step),
-                device_id_type=MESH,
-            )
-            copy.start()
-            copies_out.append(copy)
-        slots[phase, me] = mine[phase]
-        for copy in copies_out:
-            copy.wait()
-        total = slots[phase, 0]
-        for peer in range(1, peers):
-            total = total + slots[phase, peer]
-        return total
-
     def gram_of(sums, phase):
-        red[8 * tiles - 8 : 8 * tiles] = jnp.zeros((8, lanes), jnp.float32)
         for n, total in enumerate(sums):
             red[n : n + 1] = jnp.sum(total, axis=0, keepdims=True)
-        summed = jnp.sum(red[...], axis=1, keepdims=True)
-        tile = jnp.zeros((8, lanes), jnp.float32)
-        for t in range(tiles):
-            tile = jnp.where(lane_8 == t, summed[8 * t : 8 * t + 8], tile)
-        mine_x[phase] = tile
-        mine_y[phase] = exchange(
-            phase, mine_x, slots_x, gx_send, gx_recv, me_x, gx_count, ring_x
+        mine[phase] = lax.dot_general(
+            ones,
+            red[...],
+            (((1,), (1,)), ((), ())),
+            precision=lax.Precision.HIGHEST,
+            preferred_element_type=jnp.float32,
         )
-        whole = exchange(phase, mine_y, slots_y, gy_send, gy_recv, me_y, gy_count, ring_y)
-        whole = whole / total_count
-        for t in range(tiles):
-            splat[8 * t : 8 * t + 8] = jnp.broadcast_to(whole[:, t : t + 1], (8, lanes))
+        for step in range(1, devices):
+            pltpu.make_async_remote_copy(
+                src_ref=mine.at[phase, pl.ds(0, 1)],
+                dst_ref=slots.at[phase, pl.ds(me, 1)],
+                send_sem=gram_send.at[phase],
+                recv_sem=gram_recv.at[phase],
+                device_id=peer(step),
+                device_id_type=MESH,
+            ).start()
+        slots[phase, pl.ds(me, 1)] = mine[phase, 0:1]
+        every = pltpu.make_async_remote_copy(
+            src_ref=slots.at[phase, pl.ds(0, devices - 1)],
+            dst_ref=slots.at[phase, pl.ds(0, devices - 1)],
+            send_sem=gram_send.at[phase],
+            recv_sem=gram_recv.at[phase],
+            device_id=peer(1),
+            device_id_type=MESH,
+        )
+        every.wait_recv()
+        whole = jnp.sum(slots[phase], axis=0, keepdims=True) / total_count
+        spread = jnp.where(diagonal, jnp.broadcast_to(whole, diagonal.shape), 0.0)
+        splat[...] = jnp.broadcast_to(jnp.sum(spread, axis=1, keepdims=True), spread.shape)
+        every.wait_send()
         return {pair: splat[n : n + 1] for n, pair in enumerate(pairs)}
 
     def factorise(gram):
@@ -432,9 +441,10 @@
                 copy.wait_send()
 
 
-def finish(inverse_ref, basis_ref, out_ref):
+def finish(inverse_ref, basis_ref, factor_in, out_ref, factor_ref):
     count, _, depth, rows, _ = out_ref.shape
     comp, first = pl.program_id(0), pl.program_id(1) * depth
+    factor_ref[...] = factor_in[...]
 
     def one_level(level, carry):
         for half in range(rows // 8):
@@ -461,6 +471,12 @@
     coef = pltpu.VMEM((2, levels, wide, lanes), f32)
     dma = pltpu.SemaphoreType.DMA
     vmem = pl.BlockSpec(memory_space=pltpu.VMEM)
+    hbm = pl.BlockSpec(memory_space=pltpu.HBM)
+    devices = gx_count * gy_count
+    operands = [
+        pltpu.with_memory_space_constraint(x, pltpu.HBM)
+        for x in (start_vector, viscosity, friction, shifts)
+    ]
     ortho_one, factor, inverse = pl.pallas_call(
         functools.partial(kernel, gx_count, gy_count),
         out_shape=(
@@ -468,9 +484,14 @@
             jax.ShapeDtypeStruct((count, count), f32),
             jax.ShapeDtypeStruct((8 * tiles, lanes), f32),
         ),
-        in_specs=[vmem, vmem, vmem, pl.BlockSpec(memory_space=pltpu.SMEM)],
+        in_specs=[hbm] * 4,
         out_specs=(vmem, vmem, vmem),
         scratch_shapes=[
+            pltpu.VMEM(start_vector.shape, f32),
+            pltpu.VMEM(viscosity.shape, f32),
+            pltpu.VMEM(friction.shape, f32),
+            pltpu.SMEM(shifts.shape, f32),
+            dma((4,)),
             pltpu.VMEM((2, 2, 2, levels + 2, wide, lanes), f32),
             pltpu.VMEM((2, levels + 2, wide, lanes), f32),
             coef,
@@ -483,35 +504,34 @@
             coef,
             pltpu.VMEM((levels // 2, rows, lanes), f32),
             pltpu.VMEM((2, levels // 2, wide, lanes), f32),
-            pltpu.VMEM((8 * tiles, lanes), f32),
+            pltpu.VMEM((lanes, lanes), f32),
             pltpu.VMEM((2, 8, lanes), f32),
-            pltpu.VMEM((2, 8, lanes), f32),
-            pltpu.VMEM((2, gx_count, 8, lanes), f32),
-            pltpu.VMEM((2, gy_count, 8, lanes), f32),
+            pltpu.VMEM((2, devices, lanes), f32),
             pltpu.VMEM((8 * tiles, lanes), f32),
             dma((2, 3)),
             dma((2, 3)),
             dma((6,)),
             dma((6,)),
-            dma((2, gx_count)),
-            dma((2, gx_count)),
-            dma((2, gy_count)),
-            dma((2, gy_count)),
+            dma((2,)),
+            dma((2,)),
         ],
         compiler_params=pltpu.CompilerParams(
             collective_id=0, has_side_effects=True, vmem_limit_bytes=40 * 2**20
         ),
-    )(start_vector, viscosity, friction, shifts)
+    )(*operands)
     depth = 8 if levels % 8 == 0 else 1
     block = pl.BlockSpec((count, 1, depth, rows, lanes), lambda c, z: (0, c, z, 0, 0))
-    orthonormal = pl.pallas_call(
+    orthonormal, factor = pl.pallas_call(
         finish,
         grid=(2, levels // depth),
-        out_shape=jax.ShapeDtypeStruct(ortho_one.shape, f32),
-        in_specs=[vmem, vmem],
+        out_shape=(
+            jax.ShapeDtypeStruct(ortho_one.shape, f32),
+            jax.ShapeDtypeStruct(factor.shape, f32),
+        ),
+        in_specs=[vmem, vmem, vmem],
         compiler_params=pltpu.CompilerParams(vmem_limit_bytes=12 * 2**20),
-        out_specs=block,
-    )(inverse, ortho_one)
+        out_specs=(block, pl.BlockSpec(factor.shape, lambda c, z: (0, 0))),
+    )(inverse, ortho_one, factor)
     return orthonormal, factor
 
 

time: 69.8 us -> 62.3 us (0.89)
  local copies, waits for them, and re-layouts: 4 us -> 0 us
  Pallas kernels: 64.9 us -> 61.5 us
    unnamed x9 -> x0, local copies, waits for them, and re-layouts: 4 us -> none
    pallas_call x1, Pallas kernels: 62.5 us -> 59 us  [on_device(): pl.pallas_call(functools.partial(kernel, gx_count, gy_count), out_shape=(...]
where the time goes in v1:
time: 62.3 us; the launch traced here: 62.1 us
  Pallas kernels  61.5 us (99%)
  between operations  0.64 us (1%)
    pallas_call x1, Pallas kernels, on_device(): pl.pallas_call(functools.partial(kernel, gx_count, gy_count), out_shape=(...  59 us
    pallas_call x1, Pallas kernels, on_device(): pl.pallas_call(finish, grid=(2, levels // depth), out_shape=(jax.ShapeDty...  2.47 us

profile of v1, /device:TPU:0, one launch (start us, length us, event | category | flops | bytes accessed | tf_op | source)
XLA Modules:
  0.0 62.1 jit_solution(5170928275204873798)
XLA Ops:
  0.6 59.0 %shard_map.59 = (f32[9,2,16,16,128]{4,3,2,1,0:T(8,128)S(1)}, f32[9,9]{1,0:T(8,128)S(1)}, f32[48,128]{1,0:T(8,128)S(1)}) custom-call(f32[2,16,16,128]{3,2,1,0:T(8,128)} %start_hbm.1, f32[16,16,128]{2,1,0:T(8,128)} %eta_hbm.1, f32[16,16,128]{2,1,0:T(8,128)} %fric_hbm.1, f32[8]{0:T(128)} %shift_hbm.1), custom_call_target="tpu_custom_call" | custom-call | tf_op jit(solution)/shard_map/pallas_call | solution.py:480
  59.7 2.5 %shard_map.60 = (f32[9,2,16,16,128]{4,3,2,1,0:T(8,128)}, f32[9,9]{1,0:T(8,128)}) custom-call(f32[48,128]{1,0:T(8,128)S(1)} %get-tuple-element.5.inverse_ref, f32[9,2,16,16,128]{4,3,2,1,0:T(8,128)S(1)} %get-tuple-element.6.basis_ref, f32[9,9]{1,0:T(8,128)S(1)} %get-tuple-element.7.factor_in), custom_call_target="tpu_custom_call" | custom-call | tf_op jit(solution)/shard_map/pallas_call | solution.py:524

commit v2 on v1

v2 whole, which is shorter than its diff:
```python
import functools

import jax
import jax.numpy as jnp
from jax import lax
from jax.experimental import pallas as pl
from jax.experimental.pallas import tpu as pltpu
from jax.sharding import PartitionSpec as P

MESH = pl.DeviceIdType.MESH
HALO = 8
GROUP = 2 * HALO
ETA, FRIC, BASIS = 0, 1, 2
CHUNK = 4
HALVES = (slice(0, 8), slice(8, 16))


def kernel(
    gx_count,
    gy_count,
    start_hbm,
    eta_hbm,
    fric_hbm,
    shift_hbm,
    out_ref,
    factor_ref,
    lower_inv,
    loaded,
    shift_ref,
    field,
    coef,
    own,
    beside,
    pack,
    pack_eta,
    pack_coef,
    red,
    mine,
    slots,
    splat,
    load_sem,
    row_send,
    row_recv,
    side_send,
    side_recv,
    gram_send,
    gram_recv,
):
    f32 = jnp.float32
    powers = shift_hbm.shape[0]
    count = powers + 1
    levels, rows, lanes = field.shape[2], field.shape[1] - 2 * HALO, field.shape[3]
    wide = rows + 2 * HALO
    places = wide // CHUNK
    me_x, me_y = lax.axis_index("gx"), lax.axis_index("gy")
    total_count = 2.0 * levels * rows * lanes * gx_count * gy_count
    devices = gx_count * gy_count
    me = me_x * gy_count + me_y

    def peer(step):
        other = lax.rem(me + step, devices)
        return (lax.div(other, gy_count), lax.rem(other, gy_count))

    loads = [
        pltpu.make_async_copy(src, dst, load_sem.at[n])
        for n, (src, dst) in enumerate(
            (
                (eta_hbm, loaded.at[ETA]),
                (fric_hbm, loaded.at[FRIC]),
                (start_hbm, loaded.at[pl.ds(BASIS, 2)]),
                (shift_hbm, shift_ref),
            )
        )
    ]
    for load in loads:
        load.start()
    barrier = pltpu.get_barrier_semaphore()
    for step in range(1, devices):
        pl.semaphore_signal(barrier, inc=1, device_id=peer(step), device_id_type=MESH)
    for load in loads:
        load.wait()

    lane = lax.broadcasted_iota(jnp.int32, (8, lanes), 1)
    level = lax.broadcasted_iota(jnp.int32, (8, lanes), 0)
    first, last = level == 0, level == 7
    in_group = lane % GROUP
    place_of = lane // GROUP

    for x in range(rows):
        for n in range(4):
            for h in range(2):
                field[n, HALO + x, HALVES[h]] = loaded[n, pl.ds(x + rows * h, 8, stride=2 * rows)]

    pl.semaphore_wait(barrier, devices - 1)

    up_ok, down_ok = me_x > 0, me_x < gx_count - 1
    left_ok, right_ok = me_y > 0, me_y < gy_count - 1
    row_ways = (
        (down_ok, jnp.minimum(me_x + 1, gx_count - 1), rows, 0),
        (up_ok, jnp.maximum(me_x - 1, 0), HALO, rows + HALO),
    )
    side_ways = (
        (right_ok, jnp.minimum(me_y + 1, gy_count - 1)),
        (left_ok, jnp.maximum(me_y - 1, 0)),
    )

    def row_copy(way, part):
        _, other, src, dst = row_ways[way]
        return pltpu.make_async_remote_copy(
            src_ref=field.at[pl.ds(2 * part, 2), pl.ds(src, HALO)],
            dst_ref=field.at[pl.ds(2 * part, 2), pl.ds(dst, HALO)],
            send_sem=row_send.at[way, part],
            recv_sem=row_recv.at[way, part],
            device_id=(other, me_y),
            device_id_type=MESH,
        )

    def side_copy(way):
        return pltpu.make_async_remote_copy(
            src_ref=own,
            dst_ref=beside.at[way],
            send_sem=side_send.at[way],
            recv_sem=side_recv.at[way],
            device_id=(me_x, side_ways[way][1]),
            device_id_type=MESH,
        )

    for part in range(2):
        for way in range(2):

            @pl.when(row_ways[way][0])
            def _():
                row_copy(way, part).start()

    def blank(ref, shape):
        ref[ETA] = jnp.zeros(shape, f32)
        ref[FRIC] = jnp.ones(shape, f32)
        for comp in range(2):
            ref[BASIS + comp] = jnp.zeros(shape, f32)

    for way in range(2):

        @pl.when(jnp.logical_not(row_ways[1 - way][0]))
        def _():
            blank(field.at[pl.ds(0, 4), pl.ds(row_ways[way][3], HALO)], (HALO, levels, lanes))

        @pl.when(jnp.logical_not(side_ways[1 - way][0]))
        def _():
            blank(beside.at[way], (CHUNK, levels, lanes))

    def turn(value, shift):
        return pltpu.roll(value, shift % lanes, 1)

    def smooth_levels(even, odd):
        pair = even + odd
        lower = even + jnp.where(first, 0.0, pltpu.roll(odd, 1, 0))
        upper = jnp.where(last, odd, pltpu.roll(lower, 7, 0))
        return pair + lower, pair + upper

    def pairs_of(values):
        return [[a[h] + b[h] for h in range(2)] for a, b in zip(values, values[1:])]

    def coefficients(etas, frics, gates):
        sums = pairs_of(etas)
        results = []
        for r in range(len(frics)):
            smooth = smooth_levels(*[sums[r][h] + sums[r + 1][h] for h in range(2)])
            parts = []
            for h in range(2):
                here, value = etas[r + 1][h], smooth[h]
                around = (value + value) + (turn(value, 1) + turn(value, -1))
                diagonal = frics[r][h] + 6.0 * here + 0.125 * around
                g = (0.125 * gates[r]) / diagonal
                a = here * g
                parts.append(
                    (1.0 + 16.0 * a, a + a, g + g, turn(a, 1), turn(g, 1), turn(a, -1), turn(g, -1))
                )
            results.append(parts)
        return results

    def stencil(values, etas, coefs, newton):
        size = len(coefs)
        sums = [pairs_of(values[c]) for c in range(2)]
        scaled = [
            pairs_of([[e[h] * v[h] for h in range(2)] for e, v in zip(etas, values[c])])
            for c in range(2)
        ]
        results = [[None] * size for _ in range(2)]
        for r in range(size):
            crossed = []
            for c in range(2):
                slope = [sums[c][r + 1][h] - sums[c][r][h] for h in range(2)]
                crossed.append([d + d for d in slope])
            for c in range(2):
                plain = smooth_levels(*[sums[c][r][h] + sums[c][r + 1][h] for h in range(2)])
                weighted = smooth_levels(*[scaled[c][r][h] + scaled[c][r + 1][h] for h in range(2)])
                out = []
                for h in range(2):
                    centre_c, a_mid, g_mid, a_up, g_up, a_down, g_down = coefs[r](h)
                    p, q, cross = plain[h], weighted[h], crossed[1 - c][h]
                    centre = (centre_c - newton) * values[c][r + 1][h] - (a_mid * p + g_mid * q)
                    ups = a_up * (p - cross) + g_up * q
                    downs = a_down * (p + cross) + g_down * q
                    out.append(centre - (turn(ups, -1) + turn(downs, 1)))
                results[c][r] = out
        return results

    def row_of(ref, n, x):
        return [ref[n, x, half] for half in HALVES]

    def row_coefficients(start, size):
        etas = [row_of(field, ETA, start - 1 + r) for r in range(size + 2)]
        frics = [row_of(field, FRIC, start + r) for r in range(size)]
        gates = []
        for r in range(size):
            x = start + r
            inside = ((x >= HALO) | up_ok) & ((x < rows + HALO) | down_ok)
            gates.append(jnp.where(inside, 1.0, 0.0))
        for r, parts in enumerate(coefficients(etas, frics, gates)):
            for h in range(2):
                for n in range(7):
                    coef[n, start + r, HALVES[h]] = parts[h][n]

    def main_chunk(power, start):
        newton = shift_ref[power - 1]
        before = BASIS + 2 * (power - 1)
        values = [
            [row_of(field, before + c, start - 1 + r) for r in range(CHUNK + 2)] for c in range(2)
        ]
        etas = [row_of(field, ETA, start - 1 + r) for r in range(CHUNK + 2)]
        coefs = [
            lambda h, r=r: [coef[n, start + r, HALVES[h]] for n in range(7)] for r in range(CHUNK)
        ]
        results = stencil(values, etas, coefs, newton)
        for c in range(2):
            for r in range(CHUNK):
                for h in range(2):
                    field[before + 2 + c, start + r, HALVES[h]] = results[c][r][h]

    def span(power, low, high):
        def one(n, carry):
            main_chunk(power, jnp.minimum(low + CHUNK * n, high - CHUNK))
            return carry

        lax.fori_loop(0, lax.div(high - low + CHUNK - 1, CHUNK), one, 0)

    def put_own(n, g_range, fresh):
        for s in range(CHUNK):
            for half in HALVES:
                tile = jnp.zeros((8, lanes), f32) if fresh else own[n, s, half]
                for g in g_range:
                    turned = turn(field[n, CHUNK * g + s, half], GROUP * g + HALO)
                    tile = jnp.where(place_of == g, turned, tile)
                own[n, s, half] = tile

    inner_places = range(HALO // CHUNK, (HALO + rows) // CHUNK)
    outer_places = [g for g in range(places) if g not in inner_places]

    def own_inner(n, carry):
        put_own(n, inner_places, True)
        return carry

    def own_outer(n, carry):
        put_own(n, outer_places, False)
        return carry

    lax.fori_loop(0, 4, own_inner, 0)

    def inner_rows(n, carry):
        row_coefficients(HALO + 1 + n * (rows - 2 - HALO), HALO)
        return carry

    def outer_rows(n, carry):
        row_coefficients(1 + n * (rows + HALO - 2), HALO)
        return carry

    lax.fori_loop(0, 2, inner_rows, 0)

    half_way = powers // 2

    def inner_power(power, carry):
        span(power, HALO + power, HALO + rows - power)
        return carry

    lax.fori_loop(1, half_way + 1, inner_power, 0)

    for part in range(2):
        for way in range(2):

            @pl.when(row_ways[1 - way][0])
            def _():
                row_copy(way, part).wait_recv()

    lax.fori_loop(0, 4, own_outer, 0)
    for way in range(2):

        @pl.when(side_ways[way][0])
        def _():
            side_copy(way).start()

    lax.fori_loop(0, 2, outer_rows, 0)

    def outer_power(power, carry):
        def one(n, inner_carry):
            skip = lax.div(n, 2) * (rows - 2 * power)
            main_chunk(power, power + CHUNK * n + skip)
            return inner_carry

        return lax.fori_loop(0, 4, one, carry)

    lax.fori_loop(1, half_way + 1, outer_power, 0)

    for way in range(2):

        @pl.when(side_ways[1 - way][0])
        def _():
            side_copy(way).wait_recv()

    row_inside = ((place_of >= HALO // CHUNK) | up_ok) & (
        (place_of < (HALO + rows) // CHUNK) | down_ok
    )
    side_inside = (row_inside & ((in_group >= HALO) | left_ok), row_inside & ((in_group < HALO) | right_ok))
    own_part = (in_group >= HALO, in_group < HALO)

    def wrapped(values):
        return (
            [[turn(v, GROUP) for v in values[-1]]]
            + values
            + [[turn(v, -GROUP) for v in values[0]]]
        )

    for side in range(2):
        fields = [
            [
                [
                    jnp.where(own_part[side], own[n, s, half], beside[side, n, s, half])
                    for half in HALVES
                ]
                for s in range(CHUNK)
            ]
            for n in range(4)
        ]
        etas = wrapped(fields[ETA])
        gate = jnp.where(side_inside[side], 1.0, 0.0)
        for r, parts in enumerate(coefficients(etas, fields[FRIC], [gate] * CHUNK)):
            for h in range(2):
                for n in range(7):
                    pack_coef[n, side, r, HALVES[h]] = parts[h][n]
        for r in range(CHUNK + 2):
            for h in range(2):
                pack_eta[side, r, HALVES[h]] = etas[r][h]
        for c in range(2):
            for r, value in enumerate(wrapped(fields[BASIS + c])):
                for h in range(2):
                    pack[0, side, c, r, HALVES[h]] = value[h]

    edge = (lane < HALO // 2) | (lane >= lanes - HALO // 2)

    def merge(power, both, places_now):
        for c in range(2):
            for s in range(CHUNK):
                for h in range(2):
                    mixed = jnp.where(own_part[0], both[0][c][s][h], both[1][c][s][h])
                    for g in places_now:
                        x = CHUNK * g + s
                        turned = turn(mixed, -(GROUP * g + HALO))
                        spot = BASIS + 2 * power + c
                        field[spot, x, HALVES[h]] = jnp.where(
                            edge, turned, field[spot, x, HALVES[h]]
                        )

    def pack_power(power):
        newton = shift_ref[power - 1]
        now, later = lax.rem(power - 1, 2), lax.rem(power, 2)
        both = []
        for side in range(2):
            values = [
                [[pack[now, side, c, r, half] for half in HALVES] for r in range(CHUNK + 2)]
                for c in range(2)
            ]
            etas = [[pack_eta[side, r, half] for half in HALVES] for r in range(CHUNK + 2)]
            coefs = [
                lambda h, r=r: [pack_coef[n, side, r, HALVES[h]] for n in range(7)]
                for r in range(CHUNK)
            ]
            results = stencil(values, etas, coefs, newton)
            both.append(results)
            for c in range(2):
                for r, value in enumerate(wrapped(results[c])):
                    for h in range(2):
                        pack[later, side, c, r, HALVES[h]] = value[h]
        merge(power, both, inner_places)

    def early_pack(power, carry):
        pack_power(power)
        return carry

    lax.fori_loop(1, half_way + 1, early_pack, 0)

    spot = half_way % 2
    near = (in_group >= HALO + half_way, in_group < HALO - half_way)
    resync_places = range(half_way // CHUNK, (wide - half_way) // CHUNK)
    before_sync = [
        [
            [[pack[spot, side, c, 1 + s, half] for half in HALVES] for s in range(CHUNK)]
            for c in range(2)
        ]
        for side in range(2)
    ]
    for c in range(2):
        for s in range(CHUNK):
            for h in range(2):
                tile = jnp.zeros((8, lanes), f32)
                for g in resync_places:
                    turned = turn(
                        field[BASIS + 2 * half_way + c, CHUNK * g + s, HALVES[h]], GROUP * g + HALO
                    )
                    tile = jnp.where(place_of == g, turned, tile)
                for side in range(2):
                    value = jnp.where(near[side], tile, before_sync[side][c][s][h])
                    pack[spot, side, c, 1 + s, HALVES[h]] = value
                    if s == CHUNK - 1:
                        pack[spot, side, c, 0, HALVES[h]] = turn(value, GROUP)
                    if s == 0:
                        pack[spot, side, c, CHUNK + 1, HALVES[h]] = turn(value, -GROUP)
    merge(half_way, before_sync, [g for g in resync_places if g not in inner_places])

    def late_power(power, carry):
        span(power, power, wide - power)
        pack_power(power)
        return carry

    lax.fori_loop(half_way + 1, powers + 1, late_power, 0)

    pairs = [(i, j) for i in range(count) for j in range(i + 1)]
    place = {pair: n for n, pair in enumerate(pairs)}
    padded = red.shape[0]
    red[...] = jnp.zeros((padded, lanes), jnp.float32)
    ones = jnp.ones((8, lanes), jnp.float32)
    splat_rows = splat.shape[0]
    diagonal = lax.broadcasted_iota(jnp.int32, (splat_rows, lanes), 1) == lax.broadcasted_iota(
        jnp.int32, (splat_rows, lanes), 0
    )

    def add_products(sums, vectors):
        return tuple(total + vectors[i] * vectors[j] for total, (i, j) in zip(sums, pairs))

    zeros = tuple(jnp.zeros((8, lanes), jnp.float32) for _ in pairs)

    def gram_of(sums, phase):
        for n, total in enumerate(sums):
            red[n : n + 1] = jnp.sum(total, axis=0, keepdims=True)
        mine[phase] = lax.dot_general(
            ones,
            red[...],
            (((1,), (1,)), ((), ())),
            precision=lax.Precision.HIGHEST,
            preferred_element_type=jnp.float32,
        )
        for step in range(1, devices):
            pltpu.make_async_remote_copy(
                src_ref=mine.at[phase, pl.ds(0, 1)],
                dst_ref=slots.at[phase, pl.ds(me, 1)],
                send_sem=gram_send.at[phase],
                recv_sem=gram_recv.at[phase],
                device_id=peer(step),
                device_id_type=MESH,
            ).start()
        slots[phase, pl.ds(me, 1)] = mine[phase, 0:1]
        every = pltpu.make_async_remote_copy(
            src_ref=slots.at[phase, pl.ds(0, devices - 1)],
            dst_ref=slots.at[phase, pl.ds(0, devices - 1)],
            send_sem=gram_send.at[phase],
            recv_sem=gram_recv.at[phase],
            device_id=peer(1),
            device_id_type=MESH,
        )
        every.wait_recv()
        whole = jnp.sum(slots[phase], axis=0, keepdims=True) / total_count
        spread = jnp.where(diagonal, jnp.broadcast_to(whole, diagonal.shape), 0.0)
        splat[...] = jnp.broadcast_to(jnp.sum(spread, axis=1, keepdims=True), spread.shape)
        every.wait_send()
        return {pair: splat[n : n + 1] for n, pair in enumerate(pairs)}

    def factorise(gram):
        left = dict(gram)
        low, inv = {}, {}
        for j in range(count):
            root = jnp.sqrt(left[j, j])
            scale = 1.0 / root
            low[j, j], inv[j, j] = root, scale
            for i in range(j + 1, count):
                low[i, j] = left[i, j] * scale
            for i in range(j + 1, count):
                for k in range(j + 1, i + 1):
                    left[i, k] = left[i, k] - low[i, j] * low[k, j]
        for i in range(count):
            for j in range(i):
                total = low[i, j] * inv[j, j]
                for k in range(j + 1, i):
                    total = total + low[i, k] * inv[k, j]
                inv[i, j] = -(total * inv[i, i])
        for pair, n in place.items():
            lower_inv[n : n + 1] = inv[pair]
        return low

    def combine(vectors):
        results = []
        for i in range(count):
            total = lower_inv[place[i, 0] : place[i, 0] + 1] * vectors[0]
            for j in range(1, i + 1):
                total = total + lower_inv[place[i, j] : place[i, j] + 1] * vectors[j]
            results.append(total)
        return results

    def basis_at(spot, half):
        comp, x = lax.div(spot, rows), lax.rem(spot, rows)
        return [field[BASIS + 2 * n + comp, HALO + x, HALVES[half]] for n in range(count)]

    def gram_step(spot, sums):
        for half in range(2):
            sums = add_products(sums, basis_at(spot, half))
        return sums

    low_one = factorise(gram_of(lax.fori_loop(0, 2 * rows, gram_step, zeros), 0))

    def ortho_step(spot, sums):
        comp, x = lax.div(spot, rows), lax.rem(spot, rows)
        for half in range(2):
            vectors = combine(basis_at(spot, half))
            for n in range(count):
                out_ref[n, comp, x, HALVES[half]] = vectors[n]
            sums = add_products(sums, vectors)
        return sums

    low_two = factorise(gram_of(lax.fori_loop(0, 2 * rows, ortho_step, zeros), 1))

    fac_row = lax.broadcasted_iota(jnp.int32, (count, count), 0)
    fac_col = lax.broadcasted_iota(jnp.int32, (count, count), 1)
    factor = jnp.zeros((count, count), jnp.float32)
    for i in range(count):
        for j in range(i, count):
            total = low_two[i, i] * low_one[j, i]
            for k in range(i + 1, j + 1):
                total = total + low_two[k, i] * low_one[j, k]
            factor = jnp.where((fac_row == i) & (fac_col == j), total[:, :count], factor)
    factor_ref[...] = factor

    for way in range(2):

        @pl.when(row_ways[way][0])
        def _():
            for part in range(2):
                row_copy(way, part).wait_send()

        @pl.when(side_ways[way][0])
        def _():
            side_copy(way).wait_send()


def finish(inverse_ref, basis_ref, factor_in, out_ref, factor_ref):
    count, _, depth, rows, _ = out_ref.shape
    levels = basis_ref.shape[2] // rows
    comp, low = pl.program_id(0), pl.program_id(1) * depth
    factor_ref[...] = factor_in[...]

    def one_level(n, carry):
        spot_row = lax.div(low + n, 2) + 8 * lax.rem(low + n, 2)
        for half in range(rows // 8):
            part = slice(8 * half, 8 * half + 8)
            vectors = [
                basis_ref[n_basis, comp, pl.ds(8 * levels * half + spot_row, 8, stride=levels)]
                for n_basis in range(count)
            ]
            spot = 0
            for i in range(count):
                total = inverse_ref[spot : spot + 1] * vectors[0]
                for j in range(1, i + 1):
                    total = total + inverse_ref[spot + j : spot + j + 1] * vectors[j]
                out_ref[i, 0, n, part] = total
                spot += i + 1
        return carry

    lax.fori_loop(0, depth, one_level, 0)


def on_device(gx_count, gy_count, start_vector, viscosity, friction, shifts):
    levels, rows, lanes = viscosity.shape
    count = shifts.shape[0] + 1
    wide = rows + 2 * HALO
    tiles = (count * (count + 1) // 2 + 7) // 8
    f32 = jnp.float32
    dma = pltpu.SemaphoreType.DMA
    vmem = pl.BlockSpec(memory_space=pltpu.VMEM)
    hbm = pl.BlockSpec(memory_space=pltpu.HBM)
    devices = gx_count * gy_count
    flat = (levels * rows, lanes)
    operands = [
        pltpu.with_memory_space_constraint(x, pltpu.HBM)
        for x in (
            start_vector.reshape((2,) + flat),
            viscosity.reshape(flat),
            friction.reshape(flat),
            shifts,
        )
    ]
    ortho_one, factor, inverse = pl.pallas_call(
        functools.partial(kernel, gx_count, gy_count),
        out_shape=(
            jax.ShapeDtypeStruct((count, 2, rows, levels, lanes), f32),
            jax.ShapeDtypeStruct((count, count), f32),
            jax.ShapeDtypeStruct((8 * tiles, lanes), f32),
        ),
        in_specs=[hbm] * 4,
        out_specs=(vmem, vmem, vmem),
        scratch_shapes=[
            pltpu.VMEM((4,) + flat, f32),
            pltpu.SMEM(shifts.shape, f32),
            pltpu.VMEM((BASIS + 2 * count, wide, levels, lanes), f32),
            pltpu.VMEM((7, wide, levels, lanes), f32),
            pltpu.VMEM((4, CHUNK, levels, lanes), f32),
            pltpu.VMEM((2, 4, CHUNK, levels, lanes), f32),
            pltpu.VMEM((2, 2, 2, CHUNK + 2, levels, lanes), f32),
            pltpu.VMEM((2, CHUNK + 2, levels, lanes), f32),
            pltpu.VMEM((7, 2, CHUNK, levels, lanes), f32),
            pltpu.VMEM((lanes, lanes), f32),
            pltpu.VMEM((2, 8, lanes), f32),
            pltpu.VMEM((2, devices, lanes), f32),
            pltpu.VMEM((8 * tiles, lanes), f32),
            dma((4,)),
            dma((2, 2)),
            dma((2, 2)),
            dma((2,)),
            dma((2,)),
            dma((2,)),
            dma((2,)),
        ],
        compiler_params=pltpu.CompilerParams(
            collective_id=0, has_side_effects=True, vmem_limit_bytes=40 * 2**20
        ),
    )(*operands)
    depth = 8 if levels % 8 == 0 else 1
    block = pl.BlockSpec((count, 1, depth, rows, lanes), lambda c, z: (0, c, z, 0, 0))
    return tuple(
        pl.pallas_call(
            finish,
            grid=(2, levels // depth),
            out_shape=(
                jax.ShapeDtypeStruct((count,) + start_vector.shape, f32),
                jax.ShapeDtypeStruct(factor.shape, f32),
            ),
            in_specs=[vmem, vmem, vmem],
            compiler_params=pltpu.CompilerParams(vmem_limit_bytes=12 * 2**20),
            out_specs=(block, pl.BlockSpec(factor.shape, lambda c, z: (0, 0))),
        )(inverse, ortho_one.reshape(count, 2, rows * levels, lanes), factor)
    )


def solution(mesh):
    return jax.shard_map(
        functools.partial(on_device, mesh.shape["gx"], mesh.shape["gy"]),
        mesh=mesh,
        in_specs=(P(None, None, "gx", "gy"), P(None, "gx", "gy"), P(None, "gx", "gy"), P()),
        out_specs=(P(None, None, None, "gx", "gy"), P()),
        check_vma=False,
    )
```

time: 62.3 us -> 40 us (0.64)
  Pallas kernels: 61.5 us -> 39.2 us
    pallas_call x1, Pallas kernels: 59 us -> 36.2 us  [on_device(): pl.pallas_call(functools.partial(kernel, gx_count, gy_count), out_shape=(...]
where the time goes in v2:
time: 40 us; the launch traced here: 39.8 us
  Pallas kernels  39.2 us (98%)
  between operations  0.64 us (2%)
    pallas_call x1, Pallas kernels, on_device(): pl.pallas_call(functools.partial(kernel, gx_count, gy_count), out_shape=(...  36.2 us
    pallas_call x1, Pallas kernels, on_device(): pl.pallas_call(finish, grid=(2, levels // depth), out_shape=(jax.ShapeDty...  2.98 us

profile of v2, /device:TPU:0, one launch (start us, length us, event | category | flops | bytes accessed | tf_op | source)
XLA Modules:
  0.0 39.8 jit_solution(12043565140914851684)
XLA Ops:
  0.6 36.2 %shard_map.59 = (f32[9,2,16,16,128]{4,3,2,1,0:T(8,128)S(1)}, f32[9,9]{1,0:T(8,128)S(1)}, f32[48,128]{1,0:T(8,128)S(1)}) custom-call(f32[2,256,128]{2,1,0:T(8,128)} %bitcast.5, f32[256,128]{1,0:T(8,128)} %bitcast.6, f32[256,128]{1,0:T(8,128)} %bitcast.7, f32[8]{0:T(128)} %shift_hbm.1), custom_call_target="tpu_custom_call" | custom-call | tf_op jit(solution)/shard_map/pallas_call | solution.py:607
  36.9 3.0 %shard_map.60 = (f32[9,2,16,16,128]{4,3,2,1,0:T(8,128)}, f32[9,9]{1,0:T(8,128)}) custom-call(f32[48,128]{1,0:T(8,128)S(1)} %get-tuple-element.5.inverse_ref, f32[9,2,256,128]{3,2,1,0:T(8,128)S(1)} %bitcast.4, f32[9,9]{1,0:T(8,128)S(1)} %get-tuple-element.7.factor_in), custom_call_target="tpu_custom_call" | custom-call | tf_op jit(solution)/shard_map/pallas_call | solution.py:645

commit v3 on v2

--- a/solution.py
+++ b/solution.py
@@ -12,6 +12,7 @@
 GROUP = 2 * HALO
 ETA, FRIC, BASIS = 0, 1, 2
 CHUNK = 4
+NEAR = 4
 HALVES = (slice(0, 8), slice(8, 16))
 
 
@@ -30,7 +31,12 @@
     field,
     coef,
     own,
+    side_own,
+    corner_own,
     beside,
+    corner,
+    mixed,
+    sync,
     pack,
     pack_eta,
     pack_coef,
@@ -43,6 +49,8 @@
     row_recv,
     side_send,
     side_recv,
+    corner_send,
+    corner_recv,
     gram_send,
     gram_recv,
 ):
@@ -65,10 +73,14 @@
         pltpu.make_async_copy(src, dst, load_sem.at[n])
         for n, (src, dst) in enumerate(
             (
-                (eta_hbm, loaded.at[ETA]),
-                (fric_hbm, loaded.at[FRIC]),
-                (start_hbm, loaded.at[pl.ds(BASIS, 2)]),
                 (shift_hbm, shift_ref),
+                *((eta_hbm.at[:, h], loaded.at[ETA, h]) for h in range(2)),
+                *((fric_hbm.at[:, h], loaded.at[FRIC, h]) for h in range(2)),
+                *(
+                    (start_hbm.at[c, :, h], loaded.at[BASIS + c, h])
+                    for c in range(2)
+                    for h in range(2)
+                ),
             )
         )
     ]
@@ -86,18 +98,67 @@
     in_group = lane % GROUP
     place_of = lane // GROUP
 
+    flat = loaded.reshape(4, 2, 8 * rows, lanes)
     for x in range(rows):
         for n in range(4):
             for h in range(2):
-                field[n, HALO + x, HALVES[h]] = loaded[n, pl.ds(x + rows * h, 8, stride=2 * rows)]
+                field[n, HALO + x, HALVES[h]] = flat[n, h, pl.ds(x, 8, stride=rows)]
+
+    def turn(value, shift):
+        return pltpu.roll(value, shift % lanes, 1)
+
+    def gather(n, spots, tile):
+        for half in range(2):
+            tiles = tile[half]
+            for g, x in spots:
+                turned = turn(field[n, x, HALVES[half]], GROUP * g + HALO)
+                tiles = jnp.where(place_of == g, turned, tiles)
+            yield tiles
+
+    empty = [jnp.zeros((8, lanes), f32)] * 2
+    inner_places = range(HALO // CHUNK, (HALO + rows) // CHUNK)
+    outer_places = [g for g in range(places) if g not in inner_places]
+    folded = {}
+    for n in range(4):
+        for s in range(CHUNK):
+            spots = [(g, CHUNK * g + s) for g in inner_places]
+            for half, tile in enumerate(gather(n, spots, empty)):
+                own[n, s, HALVES[half]] = tile
+        for way in range(2):
+            first_row = (rows, HALO)[way]
+            spots = [
+                (2 * s + k, first_row + CHUNK * k + s) for s in range(CHUNK) for k in range(2)
+            ]
+            for half, tile in enumerate(gather(n, spots, empty)):
+                folded[way, n, half] = tile
+
+    upper_lanes = in_group >= HALO
+    inner_lanes = (place_of >= inner_places[0]) & (place_of <= inner_places[-1])
+    for n in range(4):
+        for half in HALVES:
+            two = [
+                jnp.where(inner_lanes, own[n, 2 * k, half], turn(own[n, 2 * k + 1, half], lanes // 2))
+                for k in range(2)
+            ]
+            side_own[0, n, half] = jnp.where(upper_lanes, turn(two[1], HALO), two[0])
+            side_own[1, n, half] = jnp.where(upper_lanes, two[0], turn(two[1], -HALO))
+        for way in range(2):
+            one, other = folded[way, n, 0], folded[way, n, 1]
+            corner_own[0, way, n] = jnp.where(upper_lanes, turn(other, HALO), one)
+            corner_own[1, way, n] = jnp.where(upper_lanes, one, turn(other, -HALO))
 
     pl.semaphore_wait(barrier, devices - 1)
 
     up_ok, down_ok = me_x > 0, me_x < gx_count - 1
     left_ok, right_ok = me_y > 0, me_y < gy_count - 1
     row_ways = (
-        (down_ok, jnp.minimum(me_x + 1, gx_count - 1), rows, 0),
-        (up_ok, jnp.maximum(me_x - 1, 0), HALO, rows + HALO),
+        (down_ok, jnp.minimum(me_x + 1, gx_count - 1), (rows + NEAR, rows), (NEAR, 0)),
+        (
+            up_ok,
+            jnp.maximum(me_x - 1, 0),
+            (HALO, HALO + NEAR),
+            (HALO + rows, HALO + rows + NEAR),
+        ),
     )
     side_ways = (
         (right_ok, jnp.minimum(me_y + 1, gy_count - 1)),
@@ -107,17 +168,32 @@
     def row_copy(way, part):
         _, other, src, dst = row_ways[way]
         return pltpu.make_async_remote_copy(
-            src_ref=field.at[pl.ds(2 * part, 2), pl.ds(src, HALO)],
-            dst_ref=field.at[pl.ds(2 * part, 2), pl.ds(dst, HALO)],
+            src_ref=field.at[pl.ds(0, 4), pl.ds(src[part], NEAR)],
+            dst_ref=field.at[pl.ds(0, 4), pl.ds(dst[part], NEAR)],
             send_sem=row_send.at[way, part],
             recv_sem=row_recv.at[way, part],
             device_id=(other, me_y),
             device_id_type=MESH,
         )
 
+    def corner_copy(way, side):
+        return pltpu.make_async_remote_copy(
+            src_ref=corner_own.at[side, way],
+            dst_ref=corner.at[side, way],
+            send_sem=corner_send.at[side, way],
+            recv_sem=corner_recv.at[side, way],
+            device_id=(row_ways[way][1], side_ways[side][1]),
+            device_id_type=MESH,
+        )
+
+    def corner_goes(way, side):
+        return row_ways[way][0] & side_ways[side][0]
+
+    corners = [(way, side) for way in range(2) for side in range(2)]
+
     def side_copy(way):
         return pltpu.make_async_remote_copy(
-            src_ref=own,
+            src_ref=side_own.at[way],
             dst_ref=beside.at[way],
             send_sem=side_send.at[way],
             recv_sem=side_recv.at[way],
@@ -132,6 +208,18 @@
             def _():
                 row_copy(way, part).start()
 
+    for way in range(2):
+
+        @pl.when(side_ways[way][0])
+        def _():
+            side_copy(way).start()
+
+    for way, side in corners:
+
+        @pl.when(corner_goes(way, side))
+        def _():
+            corner_copy(way, side).start()
+
     def blank(ref, shape):
         ref[ETA] = jnp.zeros(shape, f32)
         ref[FRIC] = jnp.ones(shape, f32)
@@ -142,14 +230,19 @@
 
         @pl.when(jnp.logical_not(row_ways[1 - way][0]))
         def _():
-            blank(field.at[pl.ds(0, 4), pl.ds(row_ways[way][3], HALO)], (HALO, levels, lanes))
+            blank(
+                field.at[pl.ds(0, 4), pl.ds(min(row_ways[way][3]), HALO)], (HALO, levels, lanes)
+            )
 
         @pl.when(jnp.logical_not(side_ways[1 - way][0]))
         def _():
-            blank(beside.at[way], (CHUNK, levels, lanes))
-
-    def turn(value, shift):
-        return pltpu.roll(value, shift % lanes, 1)
+            blank(beside.at[way], (levels, lanes))
+
+    for way, side in corners:
+
+        @pl.when(jnp.logical_not(corner_goes(1 - way, 1 - side)))
+        def _():
+            blank(corner.at[side, way], (8, lanes))
 
     def smooth_levels(even, odd):
         pair = even + odd
@@ -178,32 +271,51 @@
             results.append(parts)
         return results
 
-    def stencil(values, etas, coefs, newton):
-        size = len(coefs)
-        sums = [pairs_of(values[c]) for c in range(2)]
-        scaled = [
-            pairs_of([[e[h] * v[h] for h in range(2)] for e, v in zip(etas, values[c])])
-            for c in range(2)
-        ]
-        results = [[None] * size for _ in range(2)]
-        for r in range(size):
+    def stream(newton, value, eta, coefs, low, high, store, lag=2):
+        def load(r):
+            e = eta(r)
+            values = [value(c, r) for c in range(2)]
+            return values, [[e[h] * v[h] for h in range(2)] for v in values]
+
+        def add(one, two):
+            return [[[one[k][c][h] + two[k][c][h] for h in range(2)] for c in range(2)] for k in range(2)]
+
+        def finish_row(r, parts):
+            for c in range(2):
+                store(c, r, [centre - (up + down) for centre, up, down in parts[c]])
+
+        here = load(low)
+        pair = add(load(low - 1), here)
+        pending = []
+        for r in range(low, high):
+            after = load(r + 1)
+            next_pair = add(here, after)
             crossed = []
             for c in range(2):
-                slope = [sums[c][r + 1][h] - sums[c][r][h] for h in range(2)]
+                slope = [next_pair[0][c][h] - pair[0][c][h] for h in range(2)]
                 crossed.append([d + d for d in slope])
+            parts = []
             for c in range(2):
-                plain = smooth_levels(*[sums[c][r][h] + sums[c][r + 1][h] for h in range(2)])
-                weighted = smooth_levels(*[scaled[c][r][h] + scaled[c][r + 1][h] for h in range(2)])
+                plain, weighted = [
+                    smooth_levels(*[pair[k][c][h] + next_pair[k][c][h] for h in range(2)])
+                    for k in range(2)
+                ]
                 out = []
                 for h in range(2):
-                    centre_c, a_mid, g_mid, a_up, g_up, a_down, g_down = coefs[r](h)
+                    centre_c, a_mid, g_mid, a_up, g_up, a_down, g_down = coefs(r, h)
                     p, q, cross = plain[h], weighted[h], crossed[1 - c][h]
-                    centre = (centre_c - newton) * values[c][r + 1][h] - (a_mid * p + g_mid * q)
                     ups = a_up * (p - cross) + g_up * q
                     downs = a_down * (p + cross) + g_down * q
-                    out.append(centre - (turn(ups, -1) + turn(downs, 1)))
-                results[c][r] = out
-        return results
+                    up, down = turn(ups, -1), turn(downs, 1)
+                    centre = (centre_c - newton) * here[0][c][h] - (a_mid * p + g_mid * q)
+                    out.append((centre, up, down))
+                parts.append(out)
+            pending.append((r, parts))
+            if len(pending) > lag:
+                finish_row(*pending.pop(0))
+            here, pair = after, next_pair
+        for r, parts in pending:
+            finish_row(r, parts)
 
     def row_of(ref, n, x):
         return [ref[n, x, half] for half in HALVES]
@@ -221,68 +333,43 @@
                 for n in range(7):
                     coef[n, start + r, HALVES[h]] = parts[h][n]
 
-    def main_chunk(power, start):
-        newton = shift_ref[power - 1]
+    def merged(c, r, h, value):
+        turned = turn(mixed[c, r % CHUNK, HALVES[h]], -(GROUP * (r // CHUNK) + HALO))
+        return jnp.where(edge, turned, value)
+
+    def main_rows(power, low, high, merging=False):
         before = BASIS + 2 * (power - 1)
-        values = [
-            [row_of(field, before + c, start - 1 + r) for r in range(CHUNK + 2)] for c in range(2)
-        ]
-        etas = [row_of(field, ETA, start - 1 + r) for r in range(CHUNK + 2)]
-        coefs = [
-            lambda h, r=r: [coef[n, start + r, HALVES[h]] for n in range(7)] for r in range(CHUNK)
-        ]
-        results = stencil(values, etas, coefs, newton)
+
+        def store(c, r, out):
+            for h in range(2):
+                result = out[h]
+                if merging and HALO <= r < HALO + rows:
+                    result = merged(c, r, h, result)
+                field[before + 2 + c, r, HALVES[h]] = result
+
+        stream(
+            shift_ref[power - 1],
+            lambda c, r: row_of(field, before + c, r),
+            lambda r: row_of(field, ETA, r),
+            lambda r, h: [coef[n, r, HALVES[h]] for n in range(7)],
+            low,
+            high,
+            store,
+        )
+
+    def merge(power, low, high):
         for c in range(2):
-            for r in range(CHUNK):
+            for r in range(low, high):
                 for h in range(2):
-                    field[before + 2 + c, start + r, HALVES[h]] = results[c][r][h]
-
-    def span(power, low, high):
-        def one(n, carry):
-            main_chunk(power, jnp.minimum(low + CHUNK * n, high - CHUNK))
-            return carry
-
-        lax.fori_loop(0, lax.div(high - low + CHUNK - 1, CHUNK), one, 0)
-
-    def put_own(n, g_range, fresh):
-        for s in range(CHUNK):
-            for half in HALVES:
-                tile = jnp.zeros((8, lanes), f32) if fresh else own[n, s, half]
-                for g in g_range:
-                    turned = turn(field[n, CHUNK * g + s, half], GROUP * g + HALO)
-                    tile = jnp.where(place_of == g, turned, tile)
-                own[n, s, half] = tile
-
-    inner_places = range(HALO // CHUNK, (HALO + rows) // CHUNK)
-    outer_places = [g for g in range(places) if g not in inner_places]
-
-    def own_inner(n, carry):
-        put_own(n, inner_places, True)
-        return carry
-
-    def own_outer(n, carry):
-        put_own(n, outer_places, False)
-        return carry
-
-    lax.fori_loop(0, 4, own_inner, 0)
-
-    def inner_rows(n, carry):
-        row_coefficients(HALO + 1 + n * (rows - 2 - HALO), HALO)
-        return carry
-
-    def outer_rows(n, carry):
-        row_coefficients(1 + n * (rows + HALO - 2), HALO)
-        return carry
-
-    lax.fori_loop(0, 2, inner_rows, 0)
+                    spot = BASIS + 2 * power + c
+                    field[spot, r, HALVES[h]] = merged(c, r, h, field[spot, r, HALVES[h]])
+
+    row_coefficients(HALO + 1, rows - 2)
 
     half_way = powers // 2
-
-    def inner_power(power, carry):
-        span(power, HALO + power, HALO + rows - power)
-        return carry
-
-    lax.fori_loop(1, half_way + 1, inner_power, 0)
+    edge = (lane < HALO // 2) | (lane >= lanes - HALO // 2)
+    for power in range(1, half_way + 1):
+        main_rows(power, HALO + power, HALO + rows - power)
 
     for part in range(2):
         for way in range(2):
@@ -291,30 +378,25 @@
             def _():
                 row_copy(way, part).wait_recv()
 
-    lax.fori_loop(0, 4, own_outer, 0)
+        top = (NEAR, 0)[part]
+        bottom = rows + 2 * HALO - NEAR - top
+        row_coefficients(top + 1, NEAR)
+        row_coefficients(bottom - 1, NEAR)
+        for power in range(1, half_way + 1):
+            main_rows(power, top + power, top + power + NEAR)
+            main_rows(power, bottom - power, bottom - power + NEAR)
+
     for way in range(2):
 
-        @pl.when(side_ways[way][0])
-        def _():
-            side_copy(way).start()
-
-    lax.fori_loop(0, 2, outer_rows, 0)
-
-    def outer_power(power, carry):
-        def one(n, inner_carry):
-            skip = lax.div(n, 2) * (rows - 2 * power)
-            main_chunk(power, power + CHUNK * n + skip)
-            return inner_carry
-
-        return lax.fori_loop(0, 4, one, carry)
-
-    lax.fori_loop(1, half_way + 1, outer_power, 0)
-
-    for way in range(2):
-
         @pl.when(side_ways[1 - way][0])
         def _():
             side_copy(way).wait_recv()
+
+    for way, side in corners:
+
+        @pl.when(corner_goes(1 - way, 1 - side))
+        def _():
+            corner_copy(way, side).wait_recv()
 
     row_inside = ((place_of >= HALO // CHUNK) | up_ok) & (
         (place_of < (HALO + rows) // CHUNK) | down_ok
@@ -329,12 +411,36 @@
             + [[turn(v, -GROUP) for v in values[0]]]
         )
 
+    own_rows = [
+        [
+            list(
+                gather(
+                    n, [(g, CHUNK * g + s) for g in outer_places], [own[n, s, half] for half in HALVES]
+                )
+            )
+            for s in range(CHUNK)
+        ]
+        for n in range(4)
+    ]
+
+    def beside_rows(side, n, s, h):
+        back = HALO if side else -HALO
+        value = turn(beside[side, n, HALVES[h]], (s % 2) * (lanes // 2) + (s // 2) * back)
+        for way in range(2):
+            place = (0, places - HALO // CHUNK)[way]
+            turned = turn(corner[side, way, n], GROUP * (place - 2 * s) + h * back)
+            here = (place_of >= place) & (place_of < place + HALO // CHUNK)
+            value = jnp.where(here, turned, value)
+        return value
+
     for side in range(2):
         fields = [
             [
                 [
-                    jnp.where(own_part[side], own[n, s, half], beside[side, n, s, half])
-                    for half in HALVES
+                    jnp.where(
+                        own_part[side], own_rows[n][s][h], beside_rows(side, n, s, h)
+                    )
+                    for h in range(2)
                 ]
                 for s in range(CHUNK)
             ]
@@ -354,83 +460,61 @@
                 for h in range(2):
                     pack[0, side, c, r, HALVES[h]] = value[h]
 
-    edge = (lane < HALO // 2) | (lane >= lanes - HALO // 2)
-
-    def merge(power, both, places_now):
+    near = (in_group >= HALO + half_way, in_group < HALO - half_way)
+
+    def pack_power(power):
+        now, later = (power - 1) % 2, power % 2
+        results = {}
+        for side in range(2):
+
+            def store(c, r, out):
+                for h in range(2):
+                    result = out[h]
+                    results[side, c, r, h] = result
+                    if side == 1:
+                        mixed[c, r - 1, HALVES[h]] = jnp.where(
+                            own_part[0], results[0, c, r, h], result
+                        )
+                    if power == half_way:
+                        result = jnp.where(near[side], sync[c, r - 1, HALVES[h]], result)
+                    pack[later, side, c, r, HALVES[h]] = result
+                    if r == CHUNK:
+                        pack[later, side, c, 0, HALVES[h]] = turn(result, GROUP)
+                    if r == 1:
+                        pack[later, side, c, CHUNK + 1, HALVES[h]] = turn(result, -GROUP)
+
+            stream(
+                shift_ref[power - 1],
+                lambda c, r: [pack[now, side, c, r, half] for half in HALVES],
+                lambda r: [pack_eta[side, r, half] for half in HALVES],
+                lambda r, h: [pack_coef[n, side, r - 1, HALVES[h]] for n in range(7)],
+                1,
+                CHUNK + 1,
+                store,
+            )
+
+    def make_sync():
         for c in range(2):
             for s in range(CHUNK):
-                for h in range(2):
-                    mixed = jnp.where(own_part[0], both[0][c][s][h], both[1][c][s][h])
-                    for g in places_now:
-                        x = CHUNK * g + s
-                        turned = turn(mixed, -(GROUP * g + HALO))
-                        spot = BASIS + 2 * power + c
-                        field[spot, x, HALVES[h]] = jnp.where(
-                            edge, turned, field[spot, x, HALVES[h]]
+                for half in HALVES:
+                    tile = jnp.zeros((8, lanes), f32)
+                    for g in range(half_way // CHUNK, (wide - half_way) // CHUNK):
+                        turned = turn(
+                            field[BASIS + 2 * half_way + c, CHUNK * g + s, half], GROUP * g + HALO
                         )
-
-    def pack_power(power):
-        newton = shift_ref[power - 1]
-        now, later = lax.rem(power - 1, 2), lax.rem(power, 2)
-        both = []
-        for side in range(2):
-            values = [
-                [[pack[now, side, c, r, half] for half in HALVES] for r in range(CHUNK + 2)]
-                for c in range(2)
-            ]
-            etas = [[pack_eta[side, r, half] for half in HALVES] for r in range(CHUNK + 2)]
-            coefs = [
-                lambda h, r=r: [pack_coef[n, side, r, HALVES[h]] for n in range(7)]
-                for r in range(CHUNK)
-            ]
-            results = stencil(values, etas, coefs, newton)
-            both.append(results)
-            for c in range(2):
-                for r, value in enumerate(wrapped(results[c])):
-                    for h in range(2):
-                        pack[later, side, c, r, HALVES[h]] = value[h]
-        merge(power, both, inner_places)
-
-    def early_pack(power, carry):
+                        tile = jnp.where(place_of == g, turned, tile)
+                    sync[c, s, half] = tile
+
+    for power in range(1, half_way):
         pack_power(power)
-        return carry
-
-    lax.fori_loop(1, half_way + 1, early_pack, 0)
-
-    spot = half_way % 2
-    near = (in_group >= HALO + half_way, in_group < HALO - half_way)
-    resync_places = range(half_way // CHUNK, (wide - half_way) // CHUNK)
-    before_sync = [
-        [
-            [[pack[spot, side, c, 1 + s, half] for half in HALVES] for s in range(CHUNK)]
-            for c in range(2)
-        ]
-        for side in range(2)
-    ]
-    for c in range(2):
-        for s in range(CHUNK):
-            for h in range(2):
-                tile = jnp.zeros((8, lanes), f32)
-                for g in resync_places:
-                    turned = turn(
-                        field[BASIS + 2 * half_way + c, CHUNK * g + s, HALVES[h]], GROUP * g + HALO
-                    )
-                    tile = jnp.where(place_of == g, turned, tile)
-                for side in range(2):
-                    value = jnp.where(near[side], tile, before_sync[side][c][s][h])
-                    pack[spot, side, c, 1 + s, HALVES[h]] = value
-                    if s == CHUNK - 1:
-                        pack[spot, side, c, 0, HALVES[h]] = turn(value, GROUP)
-                    if s == 0:
-                        pack[spot, side, c, CHUNK + 1, HALVES[h]] = turn(value, -GROUP)
-    merge(half_way, before_sync, [g for g in resync_places if g not in inner_places])
-
-    def late_power(power, carry):
-        span(power, power, wide - power)
+        if power == half_way - 1:
+            make_sync()
+        merge(power, HALO, HALO + rows)
+    pack_power(half_way)
+    merge(half_way, half_way, wide - half_way)
+    for power in range(half_way + 1, powers + 1):
         pack_power(power)
-        return carry
-
-    lax.fori_loop(half_way + 1, powers + 1, late_power, 0)
+        main_rows(power, power, wide - power, True)
 
     pairs = [(i, j) for i in range(count) for j in range(i + 1)]
     place = {pair: n for n, pair in enumerate(pairs)}
@@ -514,26 +598,32 @@
         return results
 
     def basis_at(spot, half):
-        comp, x = lax.div(spot, rows), lax.rem(spot, rows)
+        comp, x = spot
         return [field[BASIS + 2 * n + comp, HALO + x, HALVES[half]] for n in range(count)]
 
-    def gram_step(spot, sums):
-        for half in range(2):
-            sums = add_products(sums, basis_at(spot, half))
+    def spots_of(n):
+        comp, x = lax.div(n, rows // 2), lax.rem(n, rows // 2)
+        return [(comp, 2 * x + k) for k in range(2)]
+
+    def gram_step(n, sums):
+        for spot in spots_of(n):
+            for half in range(2):
+                sums = add_products(sums, basis_at(spot, half))
         return sums
 
-    low_one = factorise(gram_of(lax.fori_loop(0, 2 * rows, gram_step, zeros), 0))
-
-    def ortho_step(spot, sums):
-        comp, x = lax.div(spot, rows), lax.rem(spot, rows)
-        for half in range(2):
-            vectors = combine(basis_at(spot, half))
-            for n in range(count):
-                out_ref[n, comp, x, HALVES[half]] = vectors[n]
-            sums = add_products(sums, vectors)
+    low_one = factorise(gram_of(lax.fori_loop(0, rows, gram_step, zeros), 0))
+
+    def ortho_step(n, sums):
+        for spot in spots_of(n):
+            comp, x = spot
+            for half in range(2):
+                vectors = combine(basis_at(spot, half))
+                for k in range(count):
+                    out_ref[k, comp, x, HALVES[half]] = vectors[k]
+                sums = add_products(sums, vectors)
         return sums
 
-    low_two = factorise(gram_of(lax.fori_loop(0, 2 * rows, ortho_step, zeros), 1))
+    low_two = factorise(gram_of(lax.fori_loop(0, rows, ortho_step, zeros), 1))
 
     fac_row = lax.broadcasted_iota(jnp.int32, (count, count), 0)
     fac_col = lax.broadcasted_iota(jnp.int32, (count, count), 1)
@@ -557,6 +647,12 @@
         def _():
             side_copy(way).wait_send()
 
+    for way, side in corners:
+
+        @pl.when(corner_goes(way, side))
+        def _():
+            corner_copy(way, side).wait_send()
+
 
 def finish(inverse_ref, basis_ref, factor_in, out_ref, factor_ref):
     count, _, depth, rows, _ = out_ref.shape
@@ -564,7 +660,7 @@
     comp, low = pl.program_id(0), pl.program_id(1) * depth
     factor_ref[...] = factor_in[...]
 
-    def one_level(n, carry):
+    def one_level(n):
         spot_row = lax.div(low + n, 2) + 8 * lax.rem(low + n, 2)
         for half in range(rows // 8):
             part = slice(8 * half, 8 * half + 8)
@@ -579,9 +675,13 @@
                     total = total + inverse_ref[spot + j : spot + j + 1] * vectors[j]
                 out_ref[i, 0, n, part] = total
                 spot += i + 1
+
+    def some_levels(n, carry):
+        for k in range(2):
+            one_level(2 * n + k)
         return carry
 
-    lax.fori_loop(0, depth, one_level, 0)
+    lax.fori_loop(0, depth // 2, some_levels, 0)
 
 
 def on_device(gx_count, gy_count, start_vector, viscosity, friction, shifts):
@@ -594,13 +694,13 @@
     vmem = pl.BlockSpec(memory_space=pltpu.VMEM)
     hbm = pl.BlockSpec(memory_space=pltpu.HBM)
     devices = gx_count * gy_count
-    flat = (levels * rows, lanes)
+    split = (levels // 2, 2, rows, lanes)
     operands = [
         pltpu.with_memory_space_constraint(x, pltpu.HBM)
         for x in (
-            start_vector.reshape((2,) + flat),
-            viscosity.reshape(flat),
-            friction.reshape(flat),
+            start_vector.reshape((2,) + split),
+            viscosity.reshape(split),
+            friction.reshape(split),
             shifts,
         )
     ]
@@ -614,12 +714,17 @@
         in_specs=[hbm] * 4,
         out_specs=(vmem, vmem, vmem),
         scratch_shapes=[
-            pltpu.VMEM((4,) + flat, f32),
+            pltpu.VMEM((4, 2, levels // 2, rows, lanes), f32),
             pltpu.SMEM(shifts.shape, f32),
             pltpu.VMEM((BASIS + 2 * count, wide, levels, lanes), f32),
             pltpu.VMEM((7, wide, levels, lanes), f32),
             pltpu.VMEM((4, CHUNK, levels, lanes), f32),
-            pltpu.VMEM((2, 4, CHUNK, levels, lanes), f32),
+            pltpu.VMEM((2, 4, levels, lanes), f32),
+            pltpu.VMEM((2, 2, 4, 8, lanes), f32),
+            pltpu.VMEM((2, 4, levels, lanes), f32),
+            pltpu.VMEM((2, 2, 4, 8, lanes), f32),
+            pltpu.VMEM((2, CHUNK, levels, lanes), f32),
+            pltpu.VMEM((2, CHUNK, levels, lanes), f32),
             pltpu.VMEM((2, 2, 2, CHUNK + 2, levels, lanes), f32),
             pltpu.VMEM((2, CHUNK + 2, levels, lanes), f32),
             pltpu.VMEM((7, 2, CHUNK, levels, lanes), f32),
@@ -627,11 +732,13 @@
             pltpu.VMEM((2, 8, lanes), f32),
             pltpu.VMEM((2, devices, lanes), f32),
             pltpu.VMEM((8 * tiles, lanes), f32),
-            dma((4,)),
+            dma((9,)),
             dma((2, 2)),
             dma((2, 2)),
             dma((2,)),
             dma((2,)),
+            dma((2, 2)),
+            dma((2, 2)),
             dma((2,)),
             dma((2,)),
         ],
@@ -639,7 +746,7 @@
             collective_id=0, has_side_effects=True, vmem_limit_bytes=40 * 2**20
         ),
     )(*operands)
-    depth = 8 if levels % 8 == 0 else 1
+    depth = 8
     block = pl.BlockSpec((count, 1, depth, rows, lanes), lambda c, z: (0, c, z, 0, 0))
     return tuple(
         pl.pallas_call(

time: 40 us -> 35.2 us (0.88)
  Pallas kernels: 39.2 us -> 34.4 us
    pallas_call x1, Pallas kernels: 36.2 us -> 31.5 us  [on_device(): pl.pallas_call(functools.partial(kernel, gx_count, gy_count), out_shape=(...]
where the time goes in v3:
time: 35.2 us; the launch traced here: 35.1 us
  Pallas kernels  34.4 us (98%)
  between operations  0.64 us (2%)
    pallas_call x1, Pallas kernels, on_device(): pl.pallas_call(functools.partial(kernel, gx_count, gy_count), out_shape=(...  31.5 us
    pallas_call x1, Pallas kernels, on_device(): pl.pallas_call(finish, grid=(2, levels // depth), out_shape=(jax.ShapeDty...  2.95 us

profile of v3, /device:TPU:0, one launch (start us, length us, event | category | flops | bytes accessed | tf_op | source)
XLA Modules:
  0.0 35.1 jit_solution(813990153097887080)
XLA Ops:
  0.6 31.5 %shard_map.59 = (f32[9,2,16,16,128]{4,3,2,1,0:T(8,128)S(1)}, f32[9,9]{1,0:T(8,128)S(1)}, f32[48,128]{1,0:T(8,128)S(1)}) custom-call(f32[2,8,2,16,128]{4,3,2,1,0:T(8,128)} %bitcast.5, f32[8,2,16,128]{3,2,1,0:T(8,128)} %bitcast.6, f32[8,2,16,128]{3,2,1,0:T(8,128)} %bitcast.7, f32[8]{0:T(128)} %shift_hbm.1), custom_call_target="tpu_custom_call" | custom-call | tf_op jit(solution)/shard_map/pallas_call | solution.py:707
  32.1 2.9 %shard_map.60 = (f32[9,2,16,16,128]{4,3,2,1,0:T(8,128)}, f32[9,9]{1,0:T(8,128)}) custom-call(f32[48,128]{1,0:T(8,128)S(1)} %get-tuple-element.5.inverse_ref, f32[9,2,256,128]{3,2,1,0:T(8,128)S(1)} %bitcast.4, f32[9,9]{1,0:T(8,128)S(1)} %get-tuple-element.7.factor_in), custom_call_target="tpu_custom_call" | custom-call | tf_op jit(solution)/shard_map/pallas_call | solution.py:752

commit v4 on v3

--- a/solution.py
+++ b/solution.py
@@ -602,8 +602,8 @@
         return [field[BASIS + 2 * n + comp, HALO + x, HALVES[half]] for n in range(count)]
 
     def spots_of(n):
-        comp, x = lax.div(n, rows // 2), lax.rem(n, rows // 2)
-        return [(comp, 2 * x + k) for k in range(2)]
+        comp, x = lax.div(n, rows // 4), lax.rem(n, rows // 4)
+        return [(comp, 4 * x + k) for k in range(4)]
 
     def gram_step(n, sums):
         for spot in spots_of(n):
@@ -611,7 +611,7 @@
                 sums = add_products(sums, basis_at(spot, half))
         return sums
 
-    low_one = factorise(gram_of(lax.fori_loop(0, rows, gram_step, zeros), 0))
+    low_one = factorise(gram_of(lax.fori_loop(0, rows // 2, gram_step, zeros), 0))
 
     def ortho_step(n, sums):
         for spot in spots_of(n):
@@ -623,7 +623,7 @@
                 sums = add_products(sums, vectors)
         return sums
 
-    low_two = factorise(gram_of(lax.fori_loop(0, rows, ortho_step, zeros), 1))
+    low_two = factorise(gram_of(lax.fori_loop(0, rows // 2, ortho_step, zeros), 1))
 
     fac_row = lax.broadcasted_iota(jnp.int32, (count, count), 0)
     fac_col = lax.broadcasted_iota(jnp.int32, (count, count), 1)
@@ -677,11 +677,11 @@
                 spot += i + 1
 
     def some_levels(n, carry):
-        for k in range(2):
-            one_level(2 * n + k)
+        for k in range(4):
+            one_level(4 * n + k)
         return carry
 
-    lax.fori_loop(0, depth // 2, some_levels, 0)
+    lax.fori_loop(0, depth // 4, some_levels, 0)
 
 
 def on_device(gx_count, gy_count, start_vector, viscosity, friction, shifts):

time: 35.2 us -> 34.9 us (level)
  no operation moved by 1% of the time
where the time goes in v4:
time: 34.9 us; the launch traced here: 34.7 us
  Pallas kernels  34.1 us (98%)
  between operations  0.64 us (2%)
    pallas_call x1, Pallas kernels, on_device(): pl.pallas_call(functools.partial(kernel, gx_count, gy_count), out_shape=(...  31.2 us
    pallas_call x1, Pallas kernels, on_device(): pl.pallas_call(finish, grid=(2, levels // depth), out_shape=(jax.ShapeDty...  2.85 us

profile of v4, /device:TPU:0, one launch (start us, length us, event | category | flops | bytes accessed | tf_op | source)
XLA Modules:
  0.0 34.7 jit_solution(16672135104406166014)
XLA Ops:
  0.6 31.2 %shard_map.59 = (f32[9,2,16,16,128]{4,3,2,1,0:T(8,128)S(1)}, f32[9,9]{1,0:T(8,128)S(1)}, f32[48,128]{1,0:T(8,128)S(1)}) custom-call(f32[2,8,2,16,128]{4,3,2,1,0:T(8,128)} %bitcast.5, f32[8,2,16,128]{3,2,1,0:T(8,128)} %bitcast.6, f32[8,2,16,128]{3,2,1,0:T(8,128)} %bitcast.7, f32[8]{0:T(128)} %shift_hbm.1), custom_call_target="tpu_custom_call" | custom-call | tf_op jit(solution)/shard_map/pallas_call | solution.py:707
  31.9 2.9 %shard_map.60 = (f32[9,2,16,16,128]{4,3,2,1,0:T(8,128)}, f32[9,9]{1,0:T(8,128)}) custom-call(f32[48,128]{1,0:T(8,128)S(1)} %get-tuple-element.5.inverse_ref, f32[9,2,256,128]{3,2,1,0:T(8,128)S(1)} %bitcast.4, f32[9,9]{1,0:T(8,128)S(1)} %get-tuple-element.7.factor_in), custom_call_target="tpu_custom_call" | custom-call | tf_op jit(solution)/shard_map/pallas_call | solution.py:752

commit v5 on v4

--- a/solution.py
+++ b/solution.py
@@ -65,9 +65,14 @@
     devices = gx_count * gy_count
     me = me_x * gy_count + me_y
 
-    def peer(step):
-        other = lax.rem(me + step, devices)
-        return (lax.div(other, gy_count), lax.rem(other, gy_count))
+    def reach(offset):
+        return min(offset[1], gy_count - offset[1]) + min(offset[0], gx_count - offset[0])
+
+    offsets = [(dx, dy) for dx in range(gx_count) for dy in range(gy_count) if dx or dy]
+    offsets.sort(key=lambda offset: -reach(offset))
+
+    def peer(offset):
+        return (lax.rem(me_x + offset[0], gx_count), lax.rem(me_y + offset[1], gy_count))
 
     loads = [
         pltpu.make_async_copy(src, dst, load_sem.at[n])
@@ -87,8 +92,8 @@
     for load in loads:
         load.start()
     barrier = pltpu.get_barrier_semaphore()
-    for step in range(1, devices):
-        pl.semaphore_signal(barrier, inc=1, device_id=peer(step), device_id_type=MESH)
+    for offset in offsets:
+        pl.semaphore_signal(barrier, inc=1, device_id=peer(offset), device_id_type=MESH)
     for load in loads:
         load.wait()
 
@@ -333,8 +338,8 @@
                 for n in range(7):
                     coef[n, start + r, HALVES[h]] = parts[h][n]
 
-    def merged(c, r, h, value):
-        turned = turn(mixed[c, r % CHUNK, HALVES[h]], -(GROUP * (r // CHUNK) + HALO))
+    def merged(power, c, r, h, value):
+        turned = turn(mixed[power, c, r % CHUNK, HALVES[h]], -(GROUP * (r // CHUNK) + HALO))
         return jnp.where(edge, turned, value)
 
     def main_rows(power, low, high, merging=False):
@@ -344,7 +349,7 @@
             for h in range(2):
                 result = out[h]
                 if merging and HALO <= r < HALO + rows:
-                    result = merged(c, r, h, result)
+                    result = merged(power, c, r, h, result)
                 field[before + 2 + c, r, HALVES[h]] = result
 
         stream(
@@ -362,7 +367,7 @@
             for r in range(low, high):
                 for h in range(2):
                     spot = BASIS + 2 * power + c
-                    field[spot, r, HALVES[h]] = merged(c, r, h, field[spot, r, HALVES[h]])
+                    field[spot, r, HALVES[h]] = merged(power, c, r, h, field[spot, r, HALVES[h]])
 
     row_coefficients(HALO + 1, rows - 2)
 
@@ -378,13 +383,12 @@
             def _():
                 row_copy(way, part).wait_recv()
 
-        top = (NEAR, 0)[part]
-        bottom = rows + 2 * HALO - NEAR - top
-        row_coefficients(top + 1, NEAR)
-        row_coefficients(bottom - 1, NEAR)
-        for power in range(1, half_way + 1):
-            main_rows(power, top + power, top + power + NEAR)
-            main_rows(power, bottom - power, bottom - power + NEAR)
+        if part == 0:
+            row_coefficients(NEAR + 1, NEAR)
+            row_coefficients(rows + HALO - 1, NEAR)
+            for power in range(1, half_way + 1):
+                main_rows(power, NEAR + power, NEAR + power + NEAR)
+                main_rows(power, rows + HALO - power, rows + HALO - power + NEAR)
 
     for way in range(2):
 
@@ -397,6 +401,10 @@
         @pl.when(corner_goes(1 - way, 1 - side))
         def _():
             corner_copy(way, side).wait_recv()
+
+    far = wide - NEAR
+    row_coefficients(1, NEAR)
+    row_coefficients(far - 1, NEAR)
 
     row_inside = ((place_of >= HALO // CHUNK) | up_ok) & (
         (place_of < (HALO + rows) // CHUNK) | down_ok
@@ -472,7 +480,7 @@
                     result = out[h]
                     results[side, c, r, h] = result
                     if side == 1:
-                        mixed[c, r - 1, HALVES[h]] = jnp.where(
+                        mixed[power, c, r - 1, HALVES[h]] = jnp.where(
                             own_part[0], results[0, c, r, h], result
                         )
                     if power == half_way:
@@ -505,16 +513,18 @@
                         tile = jnp.where(place_of == g, turned, tile)
                     sync[c, s, half] = tile
 
-    for power in range(1, half_way):
+    for power in range(1, half_way + 1):
+        main_rows(power, power, power + NEAR)
+        main_rows(power, far - power, wide - power)
+        if power == half_way:
+            make_sync()
         pack_power(power)
-        if power == half_way - 1:
-            make_sync()
-        merge(power, HALO, HALO + rows)
-    pack_power(half_way)
     merge(half_way, half_way, wide - half_way)
     for power in range(half_way + 1, powers + 1):
         pack_power(power)
         main_rows(power, power, wide - power, True)
+        if power - half_way < half_way:
+            merge(power - half_way, HALO, HALO + rows)
 
     pairs = [(i, j) for i in range(count) for j in range(i + 1)]
     place = {pair: n for n, pair in enumerate(pairs)}
@@ -541,13 +551,13 @@
             precision=lax.Precision.HIGHEST,
             preferred_element_type=jnp.float32,
         )
-        for step in range(1, devices):
+        for offset in offsets:
             pltpu.make_async_remote_copy(
                 src_ref=mine.at[phase, pl.ds(0, 1)],
                 dst_ref=slots.at[phase, pl.ds(me, 1)],
                 send_sem=gram_send.at[phase],
                 recv_sem=gram_recv.at[phase],
-                device_id=peer(step),
+                device_id=peer(offset),
                 device_id_type=MESH,
             ).start()
         slots[phase, pl.ds(me, 1)] = mine[phase, 0:1]
@@ -556,7 +566,7 @@
             dst_ref=slots.at[phase, pl.ds(0, devices - 1)],
             send_sem=gram_send.at[phase],
             recv_sem=gram_recv.at[phase],
-            device_id=peer(1),
+            device_id=peer(offsets[0]),
             device_id_type=MESH,
         )
         every.wait_recv()
@@ -723,7 +733,7 @@
             pltpu.VMEM((2, 2, 4, 8, lanes), f32),
             pltpu.VMEM((2, 4, levels, lanes), f32),
             pltpu.VMEM((2, 2, 4, 8, lanes), f32),
-            pltpu.VMEM((2, CHUNK, levels, lanes), f32),
+            pltpu.VMEM((count, 2, CHUNK, levels, lanes), f32),
             pltpu.VMEM((2, CHUNK, levels, lanes), f32),
             pltpu.VMEM((2, 2, 2, CHUNK + 2, levels, lanes), f32),
             pltpu.VMEM((2, CHUNK + 2, levels, lanes), f32),
@@ -746,7 +756,7 @@
             collective_id=0, has_side_effects=True, vmem_limit_bytes=40 * 2**20
         ),
     )(*operands)
-    depth = 8
+    depth = levels
     block = pl.BlockSpec((count, 1, depth, rows, lanes), lambda c, z: (0, c, z, 0, 0))
     return tuple(
         pl.pallas_call(

time: 34.9 us -> 34.5 us (0.989)
  Pallas kernels: 34.1 us -> 33.6 us
where the time goes in v5:
time: 34.5 us; the launch traced here: 34.3 us
  Pallas kernels  33.6 us (97%)
  between operations  0.64 us (2%)
    pallas_call x1, Pallas kernels, on_device(): pl.pallas_call(functools.partial(kernel, gx_count, gy_count), out_shape=(...  31 us
    pallas_call x1, Pallas kernels, on_device(): pl.pallas_call(finish, grid=(2, levels // depth), out_shape=(jax.ShapeDty...  2.61 us

profile of v5, /device:TPU:0, one launch (start us, length us, event | category | flops | bytes accessed | tf_op | source)
XLA Modules:
  0.0 34.3 jit_solution(11419359158071919538)
XLA Ops:
  0.6 31.0 %shard_map.59 = (f32[9,2,16,16,128]{4,3,2,1,0:T(8,128)S(1)}, f32[9,9]{1,0:T(8,128)S(1)}, f32[48,128]{1,0:T(8,128)S(1)}) custom-call(f32[2,8,2,16,128]{4,3,2,1,0:T(8,128)} %bitcast.5, f32[8,2,16,128]{3,2,1,0:T(8,128)} %bitcast.6, f32[8,2,16,128]{3,2,1,0:T(8,128)} %bitcast.7, f32[8]{0:T(128)} %shift_hbm.1), custom_call_target="tpu_custom_call" | custom-call | tf_op jit(solution)/shard_map/pallas_call | solution.py:717
  31.7 2.6 %shard_map.60 = (f32[9,2,16,16,128]{4,3,2,1,0:T(8,128)}, f32[9,9]{1,0:T(8,128)}) custom-call(f32[48,128]{1,0:T(8,128)S(1)} %get-tuple-element.5.inverse_ref, f32[9,2,256,128]{3,2,1,0:T(8,128)S(1)} %bitcast.4, f32[9,9]{1,0:T(8,128)S(1)} %get-tuple-element.7.factor_in), custom_call_target="tpu_custom_call" | custom-call | tf_op jit(solution)/shard_map/pallas_call | solution.py:762
